TPU v7x, 128 devices: a whole 4x4x4 slice. The times are simulated.
128 devices in a mesh: ctx: 8 (over z, x_lo), fsdp: 16 (over y, x_hi, core).
Axes of the slice: x: 4 (x_hi: 2, x_lo: 2; x = x_hi * 2 + x_lo), y: 4, z: 4, core: 2. Of those that a mesh axis runs over, the one named last changes fastest.
Arguments:
- inputs: bfloat16 [16, 1024, 1024], P('fsdp', 'ctx'), may hold values from -6 to 6
- segments: int32 [16, 1024], P('fsdp', 'ctx'), may hold values from 0 to 3, as said below
- routes: int32 [16, 1024, 8], P('fsdp', 'ctx'), may hold values from 0 to 31, all different within a row; in each aligned block of 128 rows (0 to 127, 128 to 255, ..., all dimensions but the last counted through in order) at most 40 rows name the same one
- gate_weights: float32 [16, 1024, 8], P('fsdp', 'ctx'), may hold values from 0.06 to 0.19
- cotangent: bfloat16 [16, 1024, 1024], P('fsdp', 'ctx'), may hold values from -6 to 6
- norm_in: bfloat16 [1024], P('fsdp'), may hold values from 0.5 to 1.5
- norm_mid: bfloat16 [1024], P('fsdp'), may hold values from 0.5 to 1.5
- q_gain: bfloat16 [64], replicated, may hold values from 0.5 to 1.5
- k_gain: bfloat16 [64], replicated, may hold values from 0.5 to 1.5
- w_query: bfloat16 [1024, 1024], P('fsdp'), may hold values from -0.1875 to 0.1875
- w_key: bfloat16 [1024, 512], P('fsdp'), may hold values from -0.1875 to 0.1875
- w_value: bfloat16 [1024, 512], P('fsdp'), may hold values from -0.1875 to 0.1875
- w_out: bfloat16 [1024, 1024], P('fsdp'), may hold values from -4 to 4
- w_gate: bfloat16 [32, 1024, 512], P('fsdp'), may hold values from -0.1875 to 0.1875
- w_up: bfloat16 [32, 1024, 512], P('fsdp'), may hold values from -0.1875 to 0.1875
- w_down: bfloat16 [32, 512, 1024], P('fsdp'), may hold values from -1.25 to 1.25
Outputs:
- output: bfloat16 [16, 1024, 1024], P('fsdp', 'ctx')
- input_grad: float32 [16, 1024, 1024], P('fsdp', 'ctx')
- grad_norm_in: float32 [1024], P('fsdp')
- grad_norm_mid: float32 [1024], P('fsdp')
- grad_q_gain: float32 [64], replicated
- grad_k_gain: float32 [64], replicated
- grad_query: float32 [1024, 1024], P('fsdp')
- grad_key: float32 [1024, 512], P('fsdp')
- grad_value: float32 [1024, 512], P('fsdp')
- grad_out: float32 [1024, 1024], P('fsdp')
- grad_gate: float32 [32, 1024, 512], P('fsdp')
- grad_up: float32 [32, 1024, 512], P('fsdp')
- grad_down: float32 [32, 512, 1024], P('fsdp')
Inputs may be any that keep to these rules, and one draw needn't show every extreme that they name: `segments`: read in the order of pos, the document numbers of a sequence never fall. `routes`: each token names 8 different experts. In every group of 128 consecutive stored rows of a sequence no expert is named by more than 40 tokens.
All inputs are finite; a program needn't handle non-finite values.
Results may differ from a plain program's by a relative error of at most 0.025.
Values may be sent and summed in bfloat16 or wider, within the bound.
A program may use at most 128 MiB of HBM per device.

v0:
```python
import math

import jax
import jax.numpy as jnp
from jax import lax
from jax.sharding import PartitionSpec as P

EXPERTS = 32
CAP = 40


def rms_scale(values, gain_vec, epsilon):
    return (
        values * lax.rsqrt(jnp.mean(values * values, axis=-1, keepdims=True) + epsilon) * gain_vec
    )


def rotary(values, positions):
    head_dim = values.shape[-1]
    half_dim = head_dim // 2
    frequency = 10000.0 ** (-jnp.arange(half_dim, dtype=jnp.float32) * 2.0 / head_dim)
    angles = positions.astype(jnp.float32)[:, None] * frequency[None, :]
    cosine = jnp.cos(angles)[:, None, :]
    sine_val = jnp.sin(angles)[:, None, :]
    front_half = values[..., :half_dim]
    back_half = values[..., half_dim:]
    return jnp.concatenate(
        [front_half * cosine - back_half * sine_val, back_half * cosine + front_half * sine_val],
        axis=-1,
    )


def slot_targets(route_rows, num_experts, capacity):
    onehot = (
        route_rows[:, :, None] == jnp.arange(num_experts, dtype=jnp.int32)[None, None, :]
    ).astype(jnp.int32)
    running = jnp.cumsum(onehot.reshape(-1, num_experts), axis=0).reshape(onehot.shape)
    slot_pos = jnp.sum(running * onehot, axis=-1) - 1
    return route_rows * capacity + slot_pos


def masked_scores(query_head, key_head, seg_local, seg_keys, score_scale):
    scores = (
        jnp.einsum("qgd,kd->gqk", query_head, key_head, preferred_element_type=jnp.float32)
        * score_scale
    )
    same_doc = (seg_local[:, None] == seg_keys[None, :])[None]
    return jnp.where(same_doc, scores, -1e30)


def head_forward(query_head, key_head, value_head, seg_local, seg_keys, score_scale):
    scores = masked_scores(query_head, key_head, seg_local, seg_keys, score_scale)
    row_peak = jnp.max(scores, axis=-1, keepdims=True)
    exp_scores = jnp.exp(scores - row_peak)
    row_total = jnp.sum(exp_scores, axis=-1, keepdims=True)
    prob_low = (exp_scores / row_total).astype(jnp.bfloat16)
    context = jnp.einsum("gqk,kd->qgd", prob_low, value_head, preferred_element_type=jnp.float32)
    return (context.astype(jnp.bfloat16), (row_peak + jnp.log(row_total))[..., 0])


def head_backward(
    query_head, key_head, value_head, grad_context, logsum, seg_local, seg_keys, score_scale
):
    scores = masked_scores(query_head, key_head, seg_local, seg_keys, score_scale)
    softmax_p = jnp.exp(scores - logsum[..., None])
    grad_probs = jnp.einsum(
        "qgd,kd->gqk", grad_context, value_head, preferred_element_type=jnp.float32
    )
    grad_value = jnp.einsum(
        "gqk,qgd->kd",
        softmax_p.astype(jnp.bfloat16),
        grad_context,
        preferred_element_type=jnp.float32,
    )
    row_inner = jnp.sum(softmax_p * grad_probs, axis=-1, keepdims=True)
    grad_scores = (softmax_p * (grad_probs - row_inner)).astype(jnp.bfloat16)
    grad_query = (
        jnp.einsum("gqk,kd->qgd", grad_scores, key_head, preferred_element_type=jnp.float32)
        * score_scale
    )
    grad_key = (
        jnp.einsum("gqk,qgd->kd", grad_scores, query_head, preferred_element_type=jnp.float32)
        * score_scale
    )
    return (grad_query.astype(jnp.bfloat16), grad_key, grad_value)


def on_device(
    inputs,
    segments,
    routes,
    gate_weights,
    cotangent,
    norm_in,
    norm_mid,
    q_gain,
    k_gain,
    w_query,
    w_key,
    w_value,
    w_out,
    w_gate,
    w_up,
    w_down,
):
    n_ctx = lax.axis_size("ctx")
    n_fsdp = lax.axis_size("fsdp")
    token_rows = inputs[0].astype(jnp.float32)
    seg_local = segments[0]
    route_local = routes[0]
    gate_local = gate_weights[0]
    grad_rows = cotangent[0].astype(jnp.float32)
    tok_count = token_rows.shape[0]
    half_rows = tok_count // 2
    width = token_rows.shape[1]
    head_dim = q_gain.shape[0]
    gain_in, gain_mid, query_full, key_full, value_full, out_full = (
        lax.all_gather(norm_in, "fsdp", axis=0, tiled=True),
        lax.all_gather(norm_mid, "fsdp", axis=0, tiled=True),
        lax.all_gather(w_query, "fsdp", axis=0, tiled=True),
        lax.all_gather(w_key, "fsdp", axis=0, tiled=True),
        lax.all_gather(w_value, "fsdp", axis=0, tiled=True),
        lax.all_gather(w_out, "fsdp", axis=0, tiled=True),
    )
    num_heads = query_full.shape[1] // head_dim
    kv_heads = key_full.shape[1] // head_dim
    groups = num_heads // kv_heads
    score_scale = 1.0 / math.sqrt(head_dim)
    ctx_index = lax.axis_index("ctx")
    local_index = jnp.arange(tok_count, dtype=jnp.int32)
    natural = jnp.where(local_index < half_rows, ctx_index, 2 * n_ctx - 1 - ctx_index)
    positions = natural * half_rows + local_index % half_rows

    def norm_first(values, gain_vec):
        return rms_scale(values, gain_vec, 1e-05)

    normed_in, pull_in = jax.vjp(norm_first, token_rows, gain_in.astype(jnp.float32))
    normed_low = normed_in.astype(jnp.bfloat16)
    query_raw = jnp.dot(normed_low, query_full, preferred_element_type=jnp.float32)
    key_raw = jnp.dot(normed_low, key_full, preferred_element_type=jnp.float32)
    value_low = jnp.dot(normed_low, value_full, preferred_element_type=jnp.float32).astype(
        jnp.bfloat16
    )

    def qk_post(query_part, key_part, gain_q, gain_k):
        query_rot = rotary(
            rms_scale(query_part.reshape(tok_count, num_heads, head_dim), gain_q, 1e-06), positions
        )
        key_rot = rotary(
            rms_scale(key_part.reshape(tok_count, kv_heads, head_dim), gain_k, 1e-06), positions
        )
        return (query_rot, key_rot)

    (query_rot, key_rot), pull_qk = jax.vjp(
        qk_post, query_raw, key_raw, q_gain.astype(jnp.float32), k_gain.astype(jnp.float32)
    )
    query_heads = (
        query_rot.astype(jnp.bfloat16)
        .reshape(tok_count, kv_heads, groups, head_dim)
        .transpose(1, 0, 2, 3)
    )
    key_low = key_rot.astype(jnp.bfloat16).reshape(tok_count, kv_heads * head_dim)
    keys_all, values_all, seg_all = (
        lax.all_gather(key_low, "ctx", axis=0, tiled=True),
        lax.all_gather(value_low, "ctx", axis=0, tiled=True),
        lax.all_gather(seg_local, "ctx", axis=0, tiled=True),
    )

    def by_head(flat):
        return flat.reshape(flat.shape[0], kv_heads, head_dim).transpose(1, 0, 2)

    def forward_head(head_items):
        return head_forward(
            head_items[0], head_items[1], head_items[2], seg_local, seg_all, score_scale
        )

    context_heads, logsum = lax.map(
        forward_head, (query_heads, by_head(keys_all), by_head(values_all))
    )
    context_low = context_heads.transpose(1, 0, 2, 3).reshape(tok_count, num_heads * head_dim)
    branch = jnp.dot(context_low, out_full, preferred_element_type=jnp.float32)
    middle = token_rows + branch
    normed_mid, pull_mid = jax.vjp(norm_first, middle, gain_mid.astype(jnp.float32))
    mid_low = normed_mid.astype(jnp.bfloat16)
    own_experts = w_gate.shape[0]
    targets = slot_targets(route_local, EXPERTS, CAP)
    slot_ids = jnp.arange(EXPERTS * CAP, dtype=jnp.int32)
    dispatch = jnp.sum(
        (targets[None, :, :] == slot_ids[:, None, None]).astype(jnp.bfloat16), axis=-1
    )
    slots_in = jnp.dot(dispatch, mid_low, preferred_element_type=jnp.float32).astype(jnp.bfloat16)
    expert_in = lax.all_to_all(
        slots_in.reshape(n_fsdp, own_experts, CAP, width),
        "fsdp",
        split_axis=0,
        concat_axis=2,
        tiled=True,
    )[0]
    gate_pre = jnp.einsum("ecd,edf->ecf", expert_in, w_gate, preferred_element_type=jnp.float32)
    up_pre = jnp.einsum("ecd,edf->ecf", expert_in, w_up, preferred_element_type=jnp.float32)

    def activate(gate_part, up_part):
        return jax.nn.silu(gate_part) * up_part

    act_out, pull_act = jax.vjp(activate, gate_pre, up_pre)
    act_low = act_out.astype(jnp.bfloat16)
    expert_out = jnp.einsum(
        "ecf,efd->ecd", act_low, w_down, preferred_element_type=jnp.float32
    ).astype(jnp.bfloat16)
    slots_out = lax.all_to_all(
        expert_out[None], "fsdp", split_axis=2, concat_axis=0, tiled=True
    ).reshape(EXPERTS * CAP, width)
    picked = slots_out[targets].astype(jnp.float32)
    combined = jnp.sum(gate_local[:, :, None] * picked, axis=1)
    output = (middle + combined).astype(jnp.bfloat16)
    weighted = (gate_local[:, :, None] * grad_rows[:, None, :]).astype(jnp.bfloat16)
    grad_slots = (
        jnp.zeros((EXPERTS * CAP, width), jnp.bfloat16)
        .at[targets.reshape(-1)]
        .add(weighted.reshape(-1, width))
    )
    grad_expert_out = lax.all_to_all(
        grad_slots.reshape(n_fsdp, own_experts, CAP, width),
        "fsdp",
        split_axis=0,
        concat_axis=2,
        tiled=True,
    )[0]
    grad_act = jnp.einsum(
        "ecd,efd->ecf", grad_expert_out, w_down, preferred_element_type=jnp.float32
    )
    grad_down = jnp.einsum(
        "ecf,ecd->efd", act_low, grad_expert_out, preferred_element_type=jnp.float32
    )
    grad_gate_pre, grad_up_pre = pull_act(grad_act)
    gate_grad_low = grad_gate_pre.astype(jnp.bfloat16)
    up_grad_low = grad_up_pre.astype(jnp.bfloat16)
    grad_gate = jnp.einsum(
        "ecd,ecf->edf", expert_in, gate_grad_low, preferred_element_type=jnp.float32
    )
    grad_up = jnp.einsum("ecd,ecf->edf", expert_in, up_grad_low, preferred_element_type=jnp.float32)
    grad_expert_in = jnp.einsum(
        "ecf,edf->ecd", gate_grad_low, w_gate, preferred_element_type=jnp.float32
    )
    grad_expert_in = grad_expert_in + jnp.einsum(
        "ecf,edf->ecd", up_grad_low, w_up, preferred_element_type=jnp.float32
    )
    grad_slots_in = lax.all_to_all(
        grad_expert_in.astype(jnp.bfloat16)[None], "fsdp", split_axis=2, concat_axis=0, tiled=True
    ).reshape(EXPERTS * CAP, width)
    grad_mid_norm = jnp.einsum(
        "sr,sd->rd", dispatch, grad_slots_in, preferred_element_type=jnp.float32
    )
    grad_gate_sum, grad_up_sum, grad_down_sum = (
        lax.psum(grad_gate.astype(jnp.bfloat16), "ctx").astype(jnp.float32),
        lax.psum(grad_up.astype(jnp.bfloat16), "ctx").astype(jnp.float32),
        lax.psum(grad_down.astype(jnp.bfloat16), "ctx").astype(jnp.float32),
    )
    grad_middle_part, grad_gain_mid = pull_mid(grad_mid_norm)
    grad_middle = grad_rows + grad_middle_part
    grad_branch = grad_middle.astype(jnp.bfloat16)
    grad_out_w = jnp.einsum(
        "rq,rd->qd", context_low, grad_branch, preferred_element_type=jnp.float32
    )
    grad_context = jnp.einsum(
        "rd,qd->rq", grad_branch, out_full, preferred_element_type=jnp.float32
    ).astype(jnp.bfloat16)
    keys_back, values_back, seg_back = (
        lax.all_gather(key_low, "ctx", axis=0, tiled=True),
        lax.all_gather(value_low, "ctx", axis=0, tiled=True),
        lax.all_gather(seg_local, "ctx", axis=0, tiled=True),
    )
    grad_context_heads = grad_context.reshape(tok_count, kv_heads, groups, head_dim).transpose(
        1, 0, 2, 3
    )

    def backward_head(head_items):
        return head_backward(
            head_items[0],
            head_items[1],
            head_items[2],
            head_items[3],
            head_items[4],
            seg_local,
            seg_back,
            score_scale,
        )

    grad_query_heads, grad_key_heads, grad_value_heads = lax.map(
        backward_head,
        (query_heads, by_head(keys_back), by_head(values_back), grad_context_heads, logsum),
    )
    grad_keys_all = grad_key_heads.transpose(1, 0, 2).reshape(-1, kv_heads * head_dim)
    grad_values_all = grad_value_heads.transpose(1, 0, 2).reshape(-1, kv_heads * head_dim)
    grad_key_rot, grad_value_sum = (
        lax.psum_scatter(
            grad_keys_all.astype(jnp.bfloat16), "ctx", scatter_dimension=0, tiled=True
        ).astype(jnp.float32),
        lax.psum_scatter(
            grad_values_all.astype(jnp.bfloat16), "ctx", scatter_dimension=0, tiled=True
        ).astype(jnp.float32),
    )
    grad_key_rot = (
        grad_key_rot.astype(jnp.bfloat16).astype(jnp.float32).reshape(tok_count, kv_heads, head_dim)
    )
    value_grad_low = grad_value_sum.astype(jnp.bfloat16)
    grad_query_rot = (
        grad_query_heads.transpose(1, 0, 2, 3)
        .reshape(tok_count, num_heads, head_dim)
        .astype(jnp.float32)
    )
    grad_query_raw, grad_key_raw, grad_q_part, grad_k_part = pull_qk((grad_query_rot, grad_key_rot))
    query_grad_low = grad_query_raw.astype(jnp.bfloat16)
    key_grad_low = grad_key_raw.astype(jnp.bfloat16)
    grad_wq = jnp.einsum(
        "rd,rq->dq", normed_low, query_grad_low, preferred_element_type=jnp.float32
    )
    grad_wk = jnp.einsum("rd,rq->dq", normed_low, key_grad_low, preferred_element_type=jnp.float32)
    grad_wv = jnp.einsum(
        "rd,rq->dq", normed_low, value_grad_low, preferred_element_type=jnp.float32
    )
    grad_normed = jnp.einsum(
        "rq,dq->rd", query_grad_low, query_full, preferred_element_type=jnp.float32
    )
    grad_normed = grad_normed + jnp.einsum(
        "rq,dq->rd", key_grad_low, key_full, preferred_element_type=jnp.float32
    )
    grad_normed = grad_normed + jnp.einsum(
        "rq,dq->rd", value_grad_low, value_full, preferred_element_type=jnp.float32
    )
    grad_input_part, grad_gain_in = pull_in(grad_normed)
    input_grad = grad_middle + grad_input_part
    grad_q_sum, grad_k_sum = lax.psum((grad_q_part, grad_k_part), ("ctx", "fsdp"))
    part_in, part_mid, part_wq, part_wk, part_wv, part_wo = (
        lax.psum_scatter(
            grad_gain_in.astype(jnp.bfloat16), "fsdp", scatter_dimension=0, tiled=True
        ).astype(jnp.float32),
        lax.psum_scatter(
            grad_gain_mid.astype(jnp.bfloat16), "fsdp", scatter_dimension=0, tiled=True
        ).astype(jnp.float32),
        lax.psum_scatter(
            grad_wq.astype(jnp.bfloat16), "fsdp", scatter_dimension=0, tiled=True
        ).astype(jnp.float32),
        lax.psum_scatter(
            grad_wk.astype(jnp.bfloat16), "fsdp", scatter_dimension=0, tiled=True
        ).astype(jnp.float32),
        lax.psum_scatter(
            grad_wv.astype(jnp.bfloat16), "fsdp", scatter_dimension=0, tiled=True
        ).astype(jnp.float32),
        lax.psum_scatter(
            grad_out_w.astype(jnp.bfloat16), "fsdp", scatter_dimension=0, tiled=True
        ).astype(jnp.float32),
    )
    sum_in, sum_mid, sum_wq, sum_wk, sum_wv, sum_wo = (
        lax.psum(part_in.astype(jnp.bfloat16), "ctx").astype(jnp.float32),
        lax.psum(part_mid.astype(jnp.bfloat16), "ctx").astype(jnp.float32),
        lax.psum(part_wq.astype(jnp.bfloat16), "ctx").astype(jnp.float32),
        lax.psum(part_wk.astype(jnp.bfloat16), "ctx").astype(jnp.float32),
        lax.psum(part_wv.astype(jnp.bfloat16), "ctx").astype(jnp.float32),
        lax.psum(part_wo.astype(jnp.bfloat16), "ctx").astype(jnp.float32),
    )
    return (
        output[None],
        input_grad[None],
        sum_in,
        sum_mid,
        grad_q_sum,
        grad_k_sum,
        sum_wq,
        sum_wk,
        sum_wv,
        sum_wo,
        grad_gate_sum,
        grad_up_sum,
        grad_down_sum,
    )


def solution(mesh):
    in_specs = (
        P("fsdp", "ctx", None),
        P("fsdp", "ctx"),
        P("fsdp", "ctx", None),
        P("fsdp", "ctx", None),
        P("fsdp", "ctx", None),
        P("fsdp"),
        P("fsdp"),
        P(),
        P(),
        P("fsdp", None),
        P("fsdp", None),
        P("fsdp", None),
        P("fsdp", None),
        P("fsdp", None, None),
        P("fsdp", None, None),
        P("fsdp", None, None),
    )
    out_specs = (
        P("fsdp", "ctx", None),
        P("fsdp", "ctx", None),
        P("fsdp"),
        P("fsdp"),
        P(),
        P(),
        P("fsdp", None),
        P("fsdp", None),
        P("fsdp", None),
        P("fsdp", None),
        P("fsdp", None, None),
        P("fsdp", None, None),
        P("fsdp", None, None),
    )
    return jax.shard_map(
        on_device, mesh=mesh, in_specs=in_specs, out_specs=out_specs, check_vma=False
    )
```

profile of v0, /device:TPU:0, one launch (start us, length us, event | category | flops | bytes accessed | tf_op | source)
XLA Modules:
  0.0 1178.4 jit_solution(11033174254715741105)
XLA Ops:
  12.4 38.8 %all-reduce.10 = (bf16[1024]{0:T(1024)(128)(2,1)S(1)}, bf16[1024]{0:T(1024)(128)(2,1)}) all-reduce(bf16[1024]{0:T(1024)(128)(2,1)S(1)} %dynamic-update-slice, bf16[1024]{0:T(1024)(128)(2,1)S(1)} %dynamic-update-slice.1), channel_id=1, replica_groups=mesh['ctx'=8,'fsdp'=16] {'fsdp'}, use_global_device_ids=true, to_apply=%add.4 | all-reduce | flops 2048 | bytes 8192
  52.3 5.4 all-gather.8.cloned.1.call-done
  57.8 2.3 convolution_convert_fusion.10
  61.6 42.2 %all-gather.12.cloned.1.call-done = bf16[1024,512]{1,0:T(8,128)(2,1)} async-done(((bf16[64,512]{1,0:T(8,128)(2,1)}), bf16[1024,512]{1,0:T(8,128)(2,1)}) %all-gather.12.cloned.1.call-update) | async-done | bytes 1048592 | tf_op jit(solution)/shard_map/all_gather | solution.py:121
  103.8 2.3 copy.119
  106.0 1.8 multiply_reduce_fusion.9
  109.0 9.0 reduce-window.6
  120.0 11.4 scatter_custom_fusion
  131.4 4.6 all-to-all-start.2
  137.1 46.2 %all-gather = s32[1,1024]{1,0:T(1,128)S(1)} all-gather(s32[1,128]{1,0:T(1,128)S(1)} %copy-done.34), channel_id=2, replica_groups=mesh['ctx'=8,'fsdp'=16] {'ctx'}, dimensions={1}, use_global_device_ids=true | all-gather | bytes 4608 | tf_op jit(solution)/shard_map/all_gather | solution.py:166
  183.4 7.4 fusion.51
  190.8 2.3 copy.118
  193.1 6.8 all-gather.16.cloned.1.call-done
  200.0 3.9 copy.120
  203.9 2.4 multiply_reduce_fusion.6
  207.3 34.0 %all-gather.14.cloned.1.call-done = bf16[1024,512]{0,1:T(8,128)(2,1)} async-done(((bf16[128,512]{0,1:T(8,128)(2,1)}), bf16[1024,512]{0,1:T(8,128)(2,1)}) %all-gather.14.cloned.1.call-update) | async-done | bytes 1048592 | tf_op jit(solution)/shard_map/all_gather | solution.py:164
  241.3 27.7 %while.26 = (s32[]{:T(128)}, bf16[8,128,2,64]{1,3,2,0:T(8,128)(2,1)S(1)}, f32[8,2,128]{2,1,0:T(2,128)}, bf16[8,1024,64]{1,2,0:T(8,128)(2,1)}, s32[1,128]{1,0:T(1...) while((s32[]{:T(128)}, ...), condition=%wide.region_6.7_spmd, body=%wide.region_3.6_spmd.sunk | while | flops 69353216 | bytes 3751005 | solution.py:177
  269.0 22.5 %all-gather.18.cloned.1.call-done = bf16[1024,1024]{1,0:T(8,128)(2,1)} async-done(((bf16[64,1024]{1,0:T(8,128)(2,1)}), bf16[1024,1024]{1,0:T(8,128)(2,1)}) %all-gather.18.cloned.1.call-update) | async-done | bytes 2097168 | tf_op jit(solution)/shard_map/all_gather | solution.py:123
  291.5 2.3 multiply_reduce_fusion.5
  294.8 2.4 convolution_convert_fusion.1
  297.2 4.7 all-to-all-start
  302.0 3.5 copy.132
  305.5 31.4 %all-to-all-done = bf16[16,2,40,1024]{3,2,1,0:T(8,128)(2,1)} async-done(((bf16[16,2,40,1024]{3,2,1,0:T(8,128)(2,1)}), bf16[16,2,40,1024]{3,2,1,0:T(8,128)(2,1)}, u32[]{:S(2)}, u32[]{:S(2)}) %all-to-all-start) | async-done | bytes 2621472 | tf_op jit(solution)/shard_map/all_to_all | solution.py:192
  336.9 2.1 copy.128
  339.3 1.5 fusion.105
  341.6 1.5 fusion.106
  343.4 3.7 multiply_convert_fusion.1
  347.1 1.6 fusion.107
  348.6 1.6 fusion.52
  350.2 4.2 copy.133
  354.4 4.9 all-to-all-start.3
  359.3 2.8 convert_bitcast_fusion
  362.2 4.2 copy.129
  366.4 27.9 %all-to-all-done.3 = bf16[1,2,640,1024]{3,1,0,2:T(2,128)(2,1)} async-done(((bf16[1,2,640,1024]{3,1,0,2:T(2,128)(2,1)}), bf16[1,2,640,1024]{3,1,0,2:T(2,128)(2,1)}, u32[]{:S(2)}, u32[]{:S(2)}) %all-to-all-start.3) | async-done | bytes 2621472 | tf_op jit(solution)/shard_map/all_to_all | solution.py:248
  394.3 4.5 all-to-all-start.1
  399.8 2.5 copy.134
  404.7 29.1 %all-to-all-done.1 = bf16[1,2,640,1024]{3,1,0,2:T(2,128)(2,1)} async-done(((bf16[1,2,640,1024]{3,1,0,2:T(2,128)(2,1)}), bf16[1,2,640,1024]{3,1,0,2:T(2,128)(2,1)}, u32[]{:S(2)}, u32[]{:S(2)}) %all-to-all-start.1) | async-done | bytes 2621472 | tf_op jit(solution)/shard_map/all_to_all | solution.py:210
  433.8 2.6 copy.130
  436.3 5.3 gather_fusion
  441.7 3.1 fusion.46
  444.8 2.1 fusion.71
  448.0 54.0 %while.27 = (s32[]{:T(128)}, bf16[8,128,2,64]{1,3,2,0:T(8,128)(2,1)S(1)}, bf16[8,1024,64]{1,2,0:T(8,128)(2,1)S(1)}, bf16[8,1024,64]{1,2,0:T(8,128)(2,1)}, bf16[8...) while((s32[]{:T(128)}, ...), condition=%wide.region_17.18_spmd, body=%wide.region_15.17_spmd.sunk | while | flops 170360576 | bytes 9222777 | solution.py:289
  477.1 1.4 multiply_reduce_fusion.11
  503.4 2.3 copy.149
  506.0 2.0 convolution_convert_fusion.5
  509.0 2.1 convolution_convert_fusion.6
  511.2 31.6 %reduce-scatter.19.cloned.1.call-done = bf16[128,512]{1,0:T(8,128)(2,1)} async-done(((bf16[1024,512]{1,0:T(8,128)(2,1)}), bf16[128,512]{1,0:T(8,128)(2,1)}) %reduce-scatter.19.cloned.1.call-update) | async-done | bytes 131088
  544.3 1.5 convolution_convert_fusion.8
  545.9 39.4 %reduce-scatter.21.cloned.1.call-done = bf16[128,512]{1,0:T(8,128)(2,1)} async-done(((bf16[1024,512]{1,0:T(8,128)(2,1)}), bf16[128,512]{1,0:T(8,128)(2,1)}) %reduce-scatter.21.cloned.1.call-update) | async-done | bytes 131088
  585.2 2.4 convolution_convert_fusion.7
  587.7 5.5 convolution_convert_fusion.3
  593.2 3.2 convolution_convert_fusion.4
  596.4 3.2 convolution_convert_fusion.2
  599.6 59.5 %reduce-scatter.17.cloned.1.call-done = bf16[64,1024]{1,0:T(8,128)(2,1)} async-done(((bf16[1024,1024]{1,0:T(8,128)(2,1)}), bf16[64,1024]{1,0:T(8,128)(2,1)}) %reduce-scatter.17.cloned.1.call-update) | async-done | bytes 131088 | tf_op jit(solution)/shard_map/reduce_scatter | solution.py:350
  659.1 74.8 %reduce-scatter.11.cloned.1.call-done = bf16[64,1024]{1,0:T(8,128)(2,1)} async-done(((bf16[1024,1024]{1,0:T(8,128)(2,1)}), bf16[64,1024]{1,0:T(8,128)(2,1)}) %reduce-scatter.11.cloned.1.call-update) | async-done | bytes 131088 | tf_op jit(solution)/shard_map/reduce_scatter | solution.py:341
  733.9 69.7 %reduce-scatter.13.cloned.1.call-done = bf16[64,512]{1,0:T(8,128)(2,1)} async-done(((bf16[1024,512]{1,0:T(8,128)(2,1)}), bf16[64,512]{1,0:T(8,128)(2,1)}) %reduce-scatter.13.cloned.1.call-update) | async-done | bytes 65552 | tf_op jit(solution)/shard_map/reduce_scatter | solution.py:344
  803.6 70.0 %reduce-scatter.15.cloned.1.call-done = bf16[64,512]{1,0:T(8,128)(2,1)} async-done(((bf16[1024,512]{1,0:T(8,128)(2,1)}), bf16[64,512]{1,0:T(8,128)(2,1)}) %reduce-scatter.15.cloned.1.call-update) | async-done | bytes 65552 | tf_op jit(solution)/shard_map/reduce_scatter | solution.py:347
  877.5 34.1 %all-reduce.9 = (bf16[1024]{0:T(1024)(128)(2,1)S(1)}, bf16[1024]{0:T(1024)(128)(2,1)S(1)}) all-reduce(bf16[1024]{0:T(1024)(128)(2,1)S(1)} %get-tuple-element.124, bf16[1024]{0:T(1024)(128)(2,1)S(1)} %get-tuple-element.122), channel_id=5, replica_groups=mesh['ctx'=8,'fsdp'=16] {'fsdp'}, use_global_device_ids=true, to_apply=%region_24.25.clone | all-reduce | flops 2048 | bytes 8192
  911.8 20.6 %all-reduce.11 = (bf16[64]{0:T(256)(128)(2,1)S(1)}, bf16[64]{0:T(256)(128)(2,1)S(1)}) all-reduce(bf16[64]{0:T(256)(128)(2,1)S(1)} %dynamic-slice.3, bf16[64]{0:T(256)(128)(2,1)S(1)} %dynamic-slice.5), channel_id=1, replica_groups=mesh['ctx'=8,'fsdp'=16] {'ctx'}, use_global_device_ids=true, to_apply=%region_25.26 | all-reduce | flops 128 | bytes 512 | tf_op jit(solution)/shard_map/psum | solution.py:355
  933.5 65.4 %all-reduce.8 = (f32[64]{0:T(128)}, f32[64]{0:T(128)}) all-reduce(f32[64]{0:T(128)S(1)} %get-tuple-element.120, f32[64]{0:T(128)S(1)} %get-tuple-element.126), channel_id=1, replica_groups=mesh['ctx'=8,'fsdp'=16] {'ctx','fsdp'}, use_global_device_ids=true, to_apply=%region_30.31 | all-reduce | flops 128 | bytes 1024 | tf_op jit(solution)/shard_map/psum | solution.py:333
  999.9 159.5 %all-reduce.15.cloned.1.call-done = (bf16[64,1024]{1,0:T(8,128)(2,1)}, bf16[64,512]{1,0:T(8,128)(2,1)}, bf16[64,512]{1,0:T(8,128)(2,1)}, bf16[64,1024]{1,0:T(8,1...) async-done(((bf16[64,1024]{1,0:T(8,128)(2,1)}, bf16[64,512]{1,0:T(8,128)(2,1)}, bf16[64,512]{1,0:T(8,128)(2,1)}, ...) | async-done | bytes 6684688 | tf_op jit(solution)/shard_map/psum | solution.py:357
  1159.4 4.3 convert_element_type.299
  1163.8 2.6 convert_element_type.301
  1166.4 2.5 convert_element_type.303
  (316 shorter events, 110.7 us)
Async XLA Ops:
  7.2 336.0 %copy-start = (bf16[2,512,1024]{2,1,0:T(8,128)(2,1)S(1)}, bf16[2,512,1024]{2,1,0:T(8,128)(2,1)}, u32[]{:S(2)}) copy-start(bf16[2,512,1024]{2,1,0:T(8,128)(2,1)} %param.35) | copy-start | bytes 6291460
  7.2 98.9 %copy-start.2 = (bf16[1,128,1024]{2,1,0:T(8,128)(2,1)S(1)}, bf16[1,128,1024]{2,1,0:T(8,128)(2,1)}, u32[]{:S(2)}) copy-start(bf16[1,128,1024]{2,1,0:T(8,128)(2,1)} %param.20) | copy-start | bytes 786436
  7.2 50.6 %all-gather.8.cloned.1.call-start = ((), (), s32[]{:S(2)}) async-start(), calls=%async_computation.10 | async-start | bytes 1114112 | tf_op jit(solution)/shard_map/all_gather | solution.py:122
  7.9 95.8 %all-gather.12.cloned.1.call-start = ((), (), s32[]{:S(2)}) async-start(), calls=%async_computation.12 | async-start | bytes 1114112 | tf_op jit(solution)/shard_map/all_gather | solution.py:121
  8.7 182.1 %all-gather.10.cloned.1.call-start = ((), (), s32[]{:S(2)}) async-start(), calls=%async_computation.11 | async-start | bytes 1179648 | tf_op jit(solution)/shard_map/all_gather | solution.py:165
  52.3 55.5 %copy-start.45 = (f32[128]{0:T(128)}, f32[128]{0:T(128)S(1)}, u32[]{:S(2)}) copy-start(f32[128]{0:T(128)S(1)} %fusion.67) | copy-start | bytes 1540
  60.1 48.6 %copy-start.43 = (s32[1,128,8]{1,2,0:T(8,128)S(1)}, s32[1,128,8]{1,2,0:T(8,128)}, u32[]{:S(2)}) copy-start(s32[1,128,8]{1,2,0:T(8,128)} %param.22) | copy-start | bytes 12292
  60.1 139.8 %all-gather.16.cloned.1.call-start = ((), (), s32[]{:S(2)}) async-start(), calls=%async_computation.14 | async-start | bytes 2228224 | tf_op jit(solution)/shard_map/all_gather | solution.py:120
  60.7 180.6 %all-gather.14.cloned.1.call-start = ((), (), s32[]{:S(2)}) async-start(), calls=%async_computation.13 | async-start | bytes 1179648 | tf_op jit(solution)/shard_map/all_gather | solution.py:164
  61.4 47.3 %copy-start.41 = (f32[64]{0:T(128)}, f32[64]{0:T(128)S(1)}, u32[]{:S(2)}) copy-start(f32[64]{0:T(128)S(1)} %convert_element_type.252) | copy-start | bytes 772
  106.0 12.7 %copy-start.35 = (f32[1,128,8]{1,2,0:T(8,128)S(1)}, f32[1,128,8]{1,2,0:T(8,128)}, u32[]{:S(2)}) copy-start(f32[1,128,8]{1,2,0:T(8,128)} %param.23) | copy-start | bytes 12292
  107.8 23.6 %copy-start.9 = (f32[128,8,64]{0,2,1:T(8,128)}, f32[128,8,64]{0,2,1:T(8,128)S(1)}, u32[]{:S(2)}) copy-start(f32[128,8,64]{0,2,1:T(8,128)S(1)} %get-tuple-element.205) | copy-start | bytes 786436
  131.4 5.2 copy-start.49
  131.4 5.7 copy-start.34
  131.4 59.4 %copy-start.44 = (bf16[1024]{0:T(1024)(128)(2,1)S(1)}, bf16[1024]{0:T(1024)(128)(2,1)}, u32[]{:S(2)}) copy-start(bf16[1024]{0:T(1024)(128)(2,1)} %get-tuple-element.171) | copy-start | bytes 6148
  131.4 165.8 %all-to-all-start.2 = ((bf16[16,2,40,1024]{3,2,1,0:T(8,128)(2,1)}), bf16[16,2,40,1024]{3,2,1,0:T(8,128)(2,1)}, u32[]{:S(2)}, u32[]{:S(2)}) async-start(bf16[16,2,40,1024]{3,2,1,0:T(8,128)(2,1)} %bitcast.321), calls=%async_computation.2 | async-start | bytes 5242880 | tf_op jit(solution)/shard_map/all_to_all | solution.py:222
  136.0 155.5 %all-gather.18.cloned.1.call-start = ((), (), s32[]{:S(2)}) async-start(), calls=%async_computation.15 | async-start | bytes 2228224 | tf_op jit(solution)/shard_map/all_gather | solution.py:123
  203.9 2.4 copy-start.37
  269.0 22.5 %copy-start.19 = (bf16[8,128,2,64]{1,3,2,0:T(8,128)(2,1)}, bf16[8,128,2,64]{1,3,2,0:T(8,128)(2,1)S(1)}, u32[]{:S(2)}) copy-start(bf16[8,128,2,64]{1,3,2,0:T(8,128)(2,1)S(1)} %get-tuple-element.115) | copy-start | bytes 786436
  291.5 3.3 copy-start.11
  293.8 108.9 %copy-start.5 = (f32[128,1024]{1,0:T(8,128)}, f32[128,1024]{1,0:T(8,128)S(1)}, u32[]{:S(2)}) copy-start(f32[128,1024]{1,0:T(8,128)S(1)} %get-tuple-element.209) | copy-start | bytes 1572868
  297.2 39.7 %all-to-all-start = ((bf16[16,2,40,1024]{3,2,1,0:T(8,128)(2,1)}), bf16[16,2,40,1024]{3,2,1,0:T(8,128)(2,1)}, u32[]{:S(2)}, u32[]{:S(2)}) async-start(bf16[16,2,40,1024]{3,2,1,0:T(8,128)(2,1)} %bitcast.322), calls=%async_computation | async-start | bytes 5242880 | tf_op jit(solution)/shard_map/all_to_all | solution.py:192
  336.9 2.4 copy-start.23
  339.1 1.8 copy-start.15
  339.3 2.3 copy-start.24
  341.6 1.7 copy-start.13
  347.1 1.6 copy-start.25
  347.1 1.6 copy-start.27
  354.4 39.9 %all-to-all-start.3 = ((bf16[1,2,640,1024]{3,1,0,2:T(2,128)(2,1)}), bf16[1,2,640,1024]{3,1,0,2:T(2,128)(2,1)}, u32[]{:S(2)}, u32[]{:S(2)}) async-start(bf16[1,2,640,1024]{3,1,0,2:T(2,128)(2,1)} %copy.133), calls=%async_computation.3 | async-start | bytes 5242880 | tf_op jit(solution)/shard_map/all_to_all | solution.py:248
  366.4 32.7 %copy-start.36 = (f32[1,128,8]{1,2,0:T(8,128)S(1)}, f32[1,128,8]{1,2,0:T(8,128)}, u32[]{:S(2)}) copy-start(f32[1,128,8]{1,2,0:T(8,128)} %param.23) | copy-start | bytes 12292
  394.3 39.5 %all-to-all-start.1 = ((bf16[1,2,640,1024]{3,1,0,2:T(2,128)(2,1)}), bf16[1,2,640,1024]{3,1,0,2:T(2,128)(2,1)}, u32[]{:S(2)}, u32[]{:S(2)}) async-start(bf16[1,2,640,1024]{3,1,0,2:T(2,128)(2,1)} %copy.129), calls=%async_computation.1 | async-start | bytes 5242880 | tf_op jit(solution)/shard_map/all_to_all | solution.py:210
  398.8 144.1 %reduce-scatter.19.cloned.1.call-start = ((), (), s32[]{:S(2)}) async-start(), calls=%async_computation.20 | async-start | bytes 1179648
  402.3 1.0 copy-start.12
  402.7 2.0 copy-start.48
  441.7 3.1 copy-start.6
  441.7 5.2 copy-start.4
  444.8 3.2 copy-start.28
  503.3 2.6 copy-start.20
  503.4 81.9 %reduce-scatter.21.cloned.1.call-start = ((), (), s32[]{:S(2)}) async-start(), calls=%async_computation.21 | async-start | bytes 1179648
  505.7 153.4 %reduce-scatter.17.cloned.1.call-start = ((), (), s32[]{:S(2)}) async-start(), calls=%async_computation.19 | async-start | bytes 2228224 | tf_op jit(solution)/shard_map/reduce_scatter | solution.py:350
  508.0 225.9 %reduce-scatter.11.cloned.1.call-start = ((), (), s32[]{:S(2)}) async-start(), calls=%async_computation.16 | async-start | bytes 2228224 | tf_op jit(solution)/shard_map/reduce_scatter | solution.py:341
  509.0 34.9 %copy-start.17 = (bf16[128,16,64]{0,2,1:T(8,128)(2,1)}, bf16[128,16,64]{0,2,1:T(8,128)(2,1)S(1)}, u32[]{:S(2)}) copy-start(bf16[128,16,64]{0,2,1:T(8,128)(2,1)S(1)} %fusion.72) | copy-start | bytes 786436
  509.0 35.0 %copy-start.10 = (f32[128,8,64]{0,2,1:T(8,128)S(1)}, f32[128,8,64]{0,2,1:T(8,128)}, u32[]{:S(2)}) copy-start(f32[128,8,64]{0,2,1:T(8,128)} %copy-done.9) | copy-start | bytes 786436
  509.0 35.0 %copy-start.42 = (f32[64]{0:T(128)S(1)}, f32[64]{0:T(128)}, u32[]{:S(2)}) copy-start(f32[64]{0:T(128)} %copy-done.41) | copy-start | bytes 772
  511.2 292.4 %reduce-scatter.13.cloned.1.call-start = ((), (), s32[]{:S(2)}) async-start(), calls=%async_computation.17 | async-start | bytes 1114112 | tf_op jit(solution)/shard_map/reduce_scatter | solution.py:344
  545.8 327.8 %reduce-scatter.15.cloned.1.call-start = ((), (), s32[]{:S(2)}) async-start(), calls=%async_computation.18 | async-start | bytes 1114112 | tf_op jit(solution)/shard_map/reduce_scatter | solution.py:347
  587.7 5.5 copy-start.26
  587.7 571.7 %all-reduce.15.cloned.1.call-start = ((), (), s32[]{:S(2)}) async-start(), calls=%async_computation.22 | async-start | bytes 13369344 | tf_op jit(solution)/shard_map/psum | solution.py:357
  587.7 5.5 copy-start.16
  593.2 3.2 copy-start.14
  593.2 3.2 copy-start.50
  873.6 1.6 copy-start.3
  873.6 1.6 copy-start.18
  873.6 3.3 copy-start.29
  875.2 1.2 copy-start.8
  875.2 1.7 copy-start.7
  876.4 122.5 %copy-start.46 = (f32[128]{0:T(128)S(1)}, f32[128]{0:T(128)}, u32[]{:S(2)}) copy-start(f32[128]{0:T(128)} %copy-done.45) | copy-start | bytes 1540
  1159.4 4.4 copy-start.22
  1163.8 2.6 copy-start.21
  1166.4 5.3 copy-start.1
  1166.4 2.5 copy-start.31
  1166.4 3.2 copy-start.30
  1166.4 4.0 copy-start.33
  1166.4 4.6 copy-start.32
  (4 other events, 2.7 us)
Sparse Core Ops, SparseCore 0:
  10.5 47.2 all-gather.7
  60.2 43.5 all-gather.11
  106.0 40.7 all-gather.9
  149.1 50.8 all-gather.15
  202.0 39.2 all-gather.13
  243.6 47.8 all-gather.17
  503.5 39.3 reduce-scatter.18
  545.3 39.9 reduce-scatter.20
  589.7 69.3 reduce-scatter.16
  663.9 69.9 reduce-scatter.10
  737.7 65.8 reduce-scatter.12
  807.7 65.8 reduce-scatter.14
  877.3 282.0 all-reduce.14
where the time goes:
time: 1190 us; the launch traced here: 1180 us
  waiting for transfers between devices  707 us (59%)
  blocking collectives  205 us (17%)
  matrix products  114 us (10%)
  other arithmetic  63.6 us (5%)
  local copies, waits for them, and re-layouts  53.2 us (4%)
  starting transfers between devices  19.4 us (2%)
  between operations  16.4 us (1%)
    psum x1, waiting for transfers between devices, on_device(): lax.psum(part_wq.astype(jnp.bfloat16), 'ctx').astype(jnp.float32)  160 us
    reduce_scatter x1, waiting for transfers between devices, on_device(): lax.psum_scatter(grad_wq.astype(jnp.bfloat16), 'fsdp', scatter_dimension=...  74.8 us
    unnamed x15, waiting for transfers between devices  73.6 us
    unnamed x2, blocking collectives  72.9 us
    reduce_scatter x1, waiting for transfers between devices, on_device(): lax.psum_scatter(grad_wv.astype(jnp.bfloat16), 'fsdp', scatter_dimension=...  70 us
    reduce_scatter x1, waiting for transfers between devices, on_device(): lax.psum_scatter(grad_wk.astype(jnp.bfloat16), 'fsdp', scatter_dimension=...  69.7 us
    psum x1, blocking collectives, on_device(): lax.psum((grad_q_part, grad_k_part), ('ctx', 'fsdp'))  65.4 us
    reduce_scatter x1, waiting for transfers between devices, on_device(): lax.psum_scatter(grad_out_w.astype(jnp.bfloat16), 'fsdp', scatter_dimensi...  59.5 us
  transfers between devices with their start and end apart: 17, of which 15 were waited for; matrix products, arithmetic and copies ran while one was open for 11% of the time, Pallas kernels for 0%

commit v1 on v0

v1 whole, which is shorter than its diff:
```python
import math

import jax
import jax.numpy as jnp
import numpy as np
from jax import lax
from jax.experimental import pallas as pl
from jax.experimental.pallas import tpu as pltpu
from jax.sharding import PartitionSpec as P

F32 = jnp.float32
BF = jnp.bfloat16
MESH = pl.DeviceIdType.MESH
EXPERTS = 32
CAP = 40
NEG = 128.0
ANY = pl.BlockSpec(memory_space=pl.ANY)
VM = pl.BlockSpec(memory_space=pltpu.VMEM)
LIMIT = 56 << 20


def dot(a, b):
    return jnp.dot(a, b, preferred_element_type=F32)


def dot_nt(a, b):
    return lax.dot_general(a, b, (((1,), (1,)), ((), ())), preferred_element_type=F32)


def dot_tn(a, b):
    return lax.dot_general(a, b, (((0,), (0,)), ((), ())), preferred_element_type=F32)


def add_low(a, b):
    return (a.astype(F32) + b.astype(F32)).astype(BF)


class Place:
    def __init__(self):
        c = lax.axis_index("ctx")
        f = lax.axis_index("fsdp")
        self.c, self.f = c, f
        self.z, self.xl = c // 2, lax.rem(c, 2)
        self.y, self.xh, self.k = f // 4, lax.rem(f // 2, 2), lax.rem(f, 2)
        self.cx = c + 1 - 2 * self.xl
        self.fx = f + 2 - 4 * self.xh
        self.z_up = (lax.rem(c + 2, 8), f)
        self.z_dn = (lax.rem(c + 6, 8), f)
        self.x_near = (self.cx, f)
        self.y_up = (c, lax.rem(f + 4, 16))
        self.y_dn = (c, lax.rem(f + 12, 16))
        self.x_far = (c, self.fx)
        self.core = (c, f + 1 - 2 * self.k)

    def ctx_peer(self, i):
        return (lax.rem(self.c + i, 8), self.f)

    def fsdp_peer(self, i):
        return (self.c, lax.rem(self.f + i, 16))


class Wire:
    def __init__(self, ssem, rsem):
        self.ssem, self.rsem = ssem, rsem
        self.started = []

    def send(self, src, dst, device):
        n = len(self.started)
        copy = pltpu.make_async_remote_copy(
            src_ref=src,
            dst_ref=dst,
            send_sem=self.ssem.at[n],
            recv_sem=self.rsem.at[n],
            device_id=device,
            device_id_type=MESH,
        )
        copy.start()
        self.started.append(copy)
        return copy

    def done(self):
        for copy in self.started:
            copy.wait_send()


def greet(devices):
    barrier = pltpu.get_barrier_semaphore()
    for device in devices:
        pl.semaphore_signal(barrier, inc=1, device_id=device, device_id_type=MESH)
    pl.semaphore_wait(barrier, len(devices))


def run_all(steps):
    steps = list(steps)
    while steps:
        alive = []
        for step in steps:
            try:
                next(step)
                alive.append(step)
            except StopIteration:
                pass
        steps = alive


def gather16(w, p, own, out, half, local):
    f, fx = p.f, p.fx
    keep = pltpu.make_async_copy(own, out.at[f], local)
    keep.start()
    from_x = w.send(own, out.at[f], p.x_far)
    rings = [(w.send(own, out.at[f], p.y_up), w.send(own, out.at[f], p.y_dn), f)]
    cores = [w.send(own, out.at[f], p.core)]
    yield
    from_x.wait_recv()
    rings.append((w.send(out.at[fx], out.at[fx], p.y_up), w.send(out.at[fx], out.at[fx], p.y_dn), fx))
    cores.append(w.send(out.at[fx], out.at[fx], p.core))
    yield
    halves = []
    for up, down, slot in rings:
        up.wait_recv()
        low = lax.rem(slot + 12, 16)
        part = out.at[low, pl.ds(0, half)]
        halves.append(w.send(part, part, p.y_up))
        cores.append(w.send(out.at[low], out.at[low], p.core))
        down.wait_recv()
        high = lax.rem(slot + 4, 16)
        part = out.at[high, pl.ds(half, own.shape[0] - half)]
        halves.append(w.send(part, part, p.y_dn))
        cores.append(w.send(out.at[high], out.at[high], p.core))
        yield
    for i, slot in ((0, f), (2, fx)):
        halves[i].wait_recv()
        halves[i + 1].wait_recv()
        far = lax.rem(slot + 8, 16)
        cores.append(w.send(out.at[far], out.at[far], p.core))
        yield
    for copy in cores:
        copy.wait_recv()
    keep.wait()


def gather8(w, p, own, out, half, local):
    c, cx = p.c, p.cx
    keep = pltpu.make_async_copy(own, out.at[c], local)
    keep.start()
    from_x = w.send(own, out.at[c], p.x_near)
    rings = [(w.send(own, out.at[c], p.z_up), w.send(own, out.at[c], p.z_dn), c)]
    yield
    from_x.wait_recv()
    rings.append((w.send(out.at[cx], out.at[cx], p.z_up), w.send(out.at[cx], out.at[cx], p.z_dn), cx))
    yield
    halves = []
    for up, down, slot in rings:
        up.wait_recv()
        part = out.at[lax.rem(slot + 6, 8), pl.ds(0, half)]
        halves.append(w.send(part, part, p.z_up))
        down.wait_recv()
        if half < own.shape[0]:
            part = out.at[lax.rem(slot + 2, 8), pl.ds(half, own.shape[0] - half)]
            halves.append(w.send(part, part, p.z_dn))
        yield
    for copy in halves:
        copy.wait_recv()
    keep.wait()


def ring_reduce(w, up, down, mine, far_up, far_down, near_up, near_down):
    a = w.send(mine(2, 0), far_up, up)
    b = w.send(mine(2, 1), far_down, down)
    c = w.send(mine(1, 1), near_up(1), up)
    d = w.send(mine(3, 0), near_down(0), down)
    yield
    a.wait_recv()
    far_up[...] = add_low(mine(1, 0)[...], far_up[...])
    e = w.send(far_up, near_up(0), up)
    b.wait_recv()
    far_down[...] = add_low(mine(3, 1)[...], far_down[...])
    g = w.send(far_down, near_down(1), down)
    yield
    for copy in (c, d, e, g):
        copy.wait_recv()


def reduce16(w, p, part, other, acc, far, near, last, finish):
    rows = part.shape[1]
    half = rows // 2
    order = (2, 1, 3, 0)
    arrivals = []
    for dy in order:
        for e in (0, 1):
            slot = lax.rem((p.f, p.fx)[e] + 4 * dy, 16) + 1 - 2 * p.k
            arrivals.append(w.send(part.at[slot], other.at[dy, e], p.core))
    yield

    def merge(i, dy):
        for e in (0, 1):
            arrivals[2 * i + e].wait_recv()
            slot = lax.rem((p.f, p.fx)[e] + 4 * dy, 16)
            acc[dy, e] = add_low(part[slot], other[dy, e])

    spans = {0: pl.ds(0, half), 1: pl.ds(half, rows - half)}

    def mine(dy, h):
        return acc.at[dy, :, spans[h]]

    for i, dy in enumerate(order[:3]):
        merge(i, dy)
    ring = ring_reduce(
        w,
        p.y_up,
        p.y_dn,
        mine,
        far.at[0],
        far.at[1],
        lambda h: near.at[0, :, spans[h]],
        lambda h: near.at[1, :, spans[h]],
    )
    next(ring)
    merge(3, 0)
    yield
    for _ in ring:
        yield
    theirs = acc[0, 1].astype(F32) + near[0, 1].astype(F32) + near[1, 1].astype(F32)
    acc[0, 1] = theirs.astype(BF)
    copy = w.send(acc.at[0, 1], last, p.x_far)
    yield
    total = acc[0, 0].astype(F32) + near[0, 0].astype(F32) + near[1, 0].astype(F32)
    copy.wait_recv()
    finish(total + last[...].astype(F32))


def reduce16_scratch(rows, cols):
    return [
        pltpu.VMEM((4, 2, rows, cols), BF),
        pltpu.VMEM((4, 2, rows, cols), BF),
        pltpu.VMEM((2, 2, rows // 2, cols), BF),
        pltpu.VMEM((2, 2, rows, cols), BF),
        pltpu.VMEM((rows, cols), BF),
    ]


def remote_params(cid):
    return pltpu.CompilerParams(collective_id=cid, has_side_effects=True, vmem_limit_bytes=LIMIT)


def local_params():
    return pltpu.CompilerParams(vmem_limit_bytes=LIMIT)


def shaped(shape, dtype):
    return jax.ShapeDtypeStruct(shape, dtype)


def first_kernel(x, seg, wp, wo, g, cot, xs, segs, wps, wos, gs, cots, ssem, rsem, local):
    p = Place()
    w = Wire(ssem, rsem)
    greet([p.z_up, p.z_dn, p.x_near, p.y_up, p.y_dn, p.x_far, p.core])
    run_all(
        [
            gather8(w, p, x, xs, 64, local.at[0]),
            gather8(w, p, seg, segs, 8, local.at[1]),
            gather16(w, p, wp, wps, 48, local.at[2]),
            gather16(w, p, wo, wos, 32, local.at[3]),
            gather16(w, p, g, gs, 16, local.at[4]),
            gather16(w, p, cot, cots, 64, local.at[5]),
        ]
    )
    w.done()


def first_gather(x, seg, wp, wo, g, cot):
    return pl.pallas_call(
        first_kernel,
        name="first_gather",
        out_shape=(
            shaped((8,) + x.shape, BF),
            shaped((8,) + seg.shape, jnp.int32),
            shaped((16,) + wp.shape, BF),
            shaped((16,) + wo.shape, BF),
            shaped((16,) + g.shape, F32),
            shaped((16,) + cot.shape, BF),
        ),
        in_specs=[ANY] * 6,
        out_specs=(ANY,) * 6,
        scratch_shapes=[
            pltpu.SemaphoreType.DMA((96,)),
            pltpu.SemaphoreType.DMA((96,)),
            pltpu.SemaphoreType.DMA((6,)),
        ],
        compiler_params=remote_params(1),
    )(x, seg, wp, wo, g, cot)


def lanes(shape):
    return lax.broadcasted_iota(jnp.int32, shape, len(shape) - 1)


def spin(v):
    first = lax.rem(lanes(v.shape), 64) < 32
    return jnp.where(first, pltpu.roll(v, 96, 1), pltpu.roll(v, 32, 1))


def head_sums(v):
    low = lanes(v.shape) < 64
    left = jnp.sum(jnp.where(low, v, 0.0), axis=-1, keepdims=True)
    right = jnp.sum(jnp.where(low, 0.0, v), axis=-1, keepdims=True)
    return jnp.where(low, left, right)


def split3(v):
    high = v.astype(BF).astype(F32)
    rest = v - high
    mid = rest.astype(BF).astype(F32)
    return high, mid, (rest - mid).astype(BF).astype(F32)


def columns3(v, base, shape):
    where = lanes(shape)
    high, mid, low = split3(v)
    return jnp.where(
        where == base, high, jnp.where(where == base + 1, mid, jnp.where(where == base + 2, low, 0.0))
    )


def attend_kernel(
    xs, segs, wps, gain, qk_gain, trig, normed, raw, qx, kx, vx, ctx_full, ctx_low, q_plain
):
    weights = wps[:, 0:64, :].reshape(1024, 256)
    place = lanes((8, 128))
    docs = lax.broadcasted_iota(jnp.int32, (8, 128), 0)
    spot = jnp.where(place == docs + 64, 1.0, 0.0)
    low = lanes((128, 128)) < 64

    def project(b, carry):
        x = xs[b].astype(F32)
        r = lax.rsqrt(jnp.mean(x * x, axis=-1, keepdims=True) + 1e-5)
        n = (x * r * gain[...]).astype(BF)
        normed[b] = n
        qkv = dot(n, weights)
        raw[b] = qkv
        q, kv = qkv[:, 0:128], qkv[:, 128:256]
        cos, sin = trig[0, b], trig[1, b]
        qn = q * lax.rsqrt(head_sums(q * q) * (1.0 / 64) + 1e-6) * qk_gain[0:1]
        q_rot = (qn * cos + spin(qn) * sin).astype(BF).astype(F32) * 0.125
        kn = kv * lax.rsqrt(head_sums(kv * kv) * (1.0 / 64) + 1e-6) * qk_gain[1:2]
        k_rot = kn * cos + spin(kn) * sin
        same = jnp.where(segs[b] == docs, 1.0, 0.0)
        doc = dot_tn(same, spot)
        bias = jnp.where((lanes((128, 128)) >= 64) & (lanes((128, 128)) < 72), (doc - 1.0) * NEG, 0.0)
        ones = jnp.where((lanes((128, 128)) >= 72) & (lanes((128, 128)) < 75), 1.0, 0.0)
        kx[b] = jnp.where(low, k_rot, doc + ones).astype(BF)
        one_v = jnp.where((lanes((128, 128)) >= 64) & (lanes((128, 128)) < 67), 1.0, 0.0)
        vx[b] = jnp.where(low, pltpu.roll(kv, 64, 1), one_v).astype(BF)
        q_plain[0, b] = jnp.where(low, q_rot, bias).astype(BF)
        q_plain[1, b] = jnp.where(low, pltpu.roll(q_rot, 64, 1), bias).astype(BF)
        return carry

    lax.fori_loop(0, 8, project, 0)
    k_all = kx[...].reshape(1024, 128)
    v_all = vx[...].reshape(1024, 128)

    def attend(b, carry):
        out = []
        for h in range(2):
            q = q_plain[h, b]
            e = jnp.exp(dot_nt(q, k_all)).astype(BF)
            o = dot(e, v_all)
            total = o[:, 64:65]
            out.append(o / total)
            keep = jnp.where(lanes((128, 128)) >= 72, 0.0, q.astype(F32))
            qx[h, b] = (keep + columns3(-jnp.log(total), 72, (128, 128))).astype(BF)
        both = jnp.where(low, out[0], pltpu.roll(out[1], 64, 1))
        ctx_full[b] = both
        ctx_low[b] = both.astype(BF)
        return carry

    lax.fori_loop(0, 8, attend, 0)


def attend(xs, segs, wps, gain, qk_gain, trig):
    return pl.pallas_call(
        attend_kernel,
        name="attend",
        out_shape=(
            shaped((8, 128, 1024), BF),
            shaped((8, 128, 256), F32),
            shaped((2, 8, 128, 128), BF),
            shaped((8, 128, 128), BF),
            shaped((8, 128, 128), BF),
            shaped((8, 128, 128), F32),
            shaped((8, 128, 128), BF),
        ),
        in_specs=[VM] * 6,
        out_specs=(VM,) * 7,
        scratch_shapes=[pltpu.VMEM((2, 8, 128, 128), BF)],
        compiler_params=local_params(),
    )(xs, segs, wps, gain, qk_gain, trig)


def middle_kernel(ctx, x, wos, gain, middle, ctx_rows, mids, rows, own, ssem, rsem, local):
    p = Place()
    w = Wire(ssem, rsem)
    greet([p.ctx_peer(i) for i in range(1, 8)] + [p.y_up, p.y_dn, p.x_far, p.core])
    place = pl.ds(pl.multiple_of(p.c * 128, 128), 128)
    keep = pltpu.make_async_copy(ctx.at[p.c], rows.at[:, place], local.at[0])
    keep.start()
    arrivals = []
    for i in range(1, 8):
        to = lax.rem(p.c + i, 8)
        arrivals.append(w.send(ctx.at[to], rows.at[:, place], (to, p.f)))
    keep.wait()
    for copy in arrivals:
        copy.wait_recv()
    for t in range(4):
        cols = slice(256 * t, 256 * t + 256)
        middle[:, cols] = x[:, cols].astype(F32) + dot(rows[...], wos[:, cols])
    m = middle[...]
    r = lax.rsqrt(jnp.mean(m * m, axis=-1, keepdims=True) + 1e-5)
    own[...] = (m * r * gain[...]).astype(BF)
    ctx_rows[...] = rows[...]
    run_all([gather16(w, p, own, mids, 64, local.at[1])])
    w.done()


def middle_gather(ctx, x, wos, gain):
    return pl.pallas_call(
        middle_kernel,
        name="middle_gather",
        out_shape=(
            shaped((128, 1024), F32),
            shaped((128, 1024), BF),
            shaped((16, 128, 1024), BF),
        ),
        in_specs=[ANY, VM, VM, VM],
        out_specs=(VM, VM, ANY),
        scratch_shapes=[
            pltpu.VMEM((128, 1024), BF),
            pltpu.VMEM((128, 1024), BF),
            pltpu.SemaphoreType.DMA((32,)),
            pltpu.SemaphoreType.DMA((32,)),
            pltpu.SemaphoreType.DMA((2,)),
        ],
        compiler_params=remote_params(2),
    )(ctx, x, wos, gain)


def expert_kernel(
    gs, mids, cots, wg, wu, wd,
    outs, grads, dg, du, dd,
    table, key, hot, xin, gout, gate, act, ggp, gup, yo, yi,
):
    f = lax.axis_index("fsdp")
    for s in range(16):
        table[2 * s : 2 * s + 2, :] = gs[s, pl.ds(2 * f, 2), :]
    named = table[...] > 0.0
    row = lax.broadcasted_iota(jnp.int32, (128, 128), 0)
    col = lax.broadcasted_iota(jnp.int32, (128, 128), 1)
    before = jnp.where(row < col, 1.0, 0.0).astype(BF)
    count = dot(jnp.where(named, 1.0, 0.0).astype(BF), before)
    odd = lax.rem(lax.broadcasted_iota(jnp.int32, (32, 128), 0) // 2, 2).astype(F32)
    key[...] = jnp.where(named, count + odd * CAP, -1.0)
    slot = lax.broadcasted_iota(jnp.int32, (2 * CAP, 256), 0).astype(F32)

    for q in range(8):
        pair = mids[2 * q : 2 * q + 2].reshape(256, 1024)
        cot = cots[2 * q : 2 * q + 2].reshape(256, 1024)
        rows = slice(2 * CAP * q, 2 * CAP * q + 2 * CAP)
        for j in range(2):
            a, b = 4 * q + j, 4 * q + 2 + j
            keys = jnp.concatenate([key[a : a + 1, :], key[b : b + 1, :]], axis=1)
            vals = jnp.concatenate([table[a : a + 1, :], table[b : b + 1, :]], axis=1)
            chosen = slot == keys
            hot[q, j] = jnp.where(chosen, 1.0, 0.0).astype(BF)
            weight = jnp.sum(jnp.where(chosen, vals, 0.0), axis=1, keepdims=True)
            gate[j, rows, :] = jnp.broadcast_to(weight, (2 * CAP, 128))
            xin[j, rows, :] = dot(hot[q, j], pair).astype(BF)
            gout[j, rows, :] = (weight * dot(hot[q, j], cot)).astype(BF)

    for j in range(2):

        def rows_step(t, carry, j=j):
            rows = pl.ds(pl.multiple_of(t * 128, 128), 128)
            x = xin[j, rows, :]
            go = gout[j, rows, :]
            gp = dot(x, wg[j])
            up = dot(x, wu[j])
            s = 1.0 / (1.0 + jnp.exp(-gp))
            silu = gp * s
            a = (silu * up).astype(BF)
            act[rows, :] = a
            eo = dot(a, wd[j])
            yo[j, rows, :] = (gate[j, rows, 0:1] * eo).astype(BF)
            ga = dot_nt(go, wd[j])
            gg = (ga * up * (s * (1.0 + gp * (1.0 - s)))).astype(BF)
            gu = (ga * silu).astype(BF)
            ggp[rows, :] = gg
            gup[rows, :] = gu
            yi[j, rows, :] = (dot_nt(gg, wg[j]) + dot_nt(gu, wu[j])).astype(BF)
            return carry

        lax.fori_loop(0, 5, rows_step, 0)

        def grads_step(t, carry, j=j):
            cols = pl.ds(pl.multiple_of(t * 256, 256), 256)
            x = xin[j, :, cols]
            dg[j, cols, :] = dot_tn(x, ggp[...]).astype(BF)
            du[j, cols, :] = dot_tn(x, gup[...]).astype(BF)
            dd[j, :, cols] = dot_tn(act[...], gout[j, :, cols]).astype(BF)
            return carry

        lax.fori_loop(0, 4, grads_step, 0)

    for q in range(8):
        rows = slice(2 * CAP * q, 2 * CAP * q + 2 * CAP)
        o = dot_tn(hot[q, 0], yo[0, rows, :]) + dot_tn(hot[q, 1], yo[1, rows, :])
        outs[2 * q : 2 * q + 2] = o.astype(BF).reshape(2, 128, 1024)
        g = dot_tn(hot[q, 0], yi[0, rows, :]) + dot_tn(hot[q, 1], yi[1, rows, :])
        grads[2 * q : 2 * q + 2] = g.astype(BF).reshape(2, 128, 1024)


def experts(gs, mids, cots, wg, wu, wd):
    slots = 16 * CAP
    return pl.pallas_call(
        expert_kernel,
        name="experts",
        out_shape=(
            shaped((16, 128, 1024), BF),
            shaped((16, 128, 1024), BF),
            shaped((2, 1024, 512), BF),
            shaped((2, 1024, 512), BF),
            shaped((2, 512, 1024), BF),
        ),
        in_specs=[VM] * 6,
        out_specs=(VM,) * 5,
        scratch_shapes=[
            pltpu.VMEM((32, 128), F32),
            pltpu.VMEM((32, 128), F32),
            pltpu.VMEM((8, 2, 2 * CAP, 256), BF),
            pltpu.VMEM((2, slots, 1024), BF),
            pltpu.VMEM((2, slots, 1024), BF),
            pltpu.VMEM((2, slots, 128), F32),
            pltpu.VMEM((slots, 512), BF),
            pltpu.VMEM((slots, 512), BF),
            pltpu.VMEM((slots, 512), BF),
            pltpu.VMEM((2, slots, 1024), BF),
            pltpu.VMEM((2, slots, 1024), BF),
        ],
        compiler_params=local_params(),
    )(gs, mids, cots, wg, wu, wd)


def return_kernel(
    grads, outs, dg, du, dd, middle, cot, wos, gain, ctx_rows,
    output, grad_middle, grad_gain, dctx, grad_out, own_g, own_u, own_d,
    go, ga, gf, gn, gl, oo, oa, of, on, ol,
    gfar, gnear, gx, ufar, unear, ux, dmine, dx, dfar, dnear,
    total, branch, back, ssem, rsem, local,
):
    p = Place()
    w = Wire(ssem, rsem)
    greet(
        [p.ctx_peer(i) for i in range(1, 8)]
        + [p.y_up, p.y_dn, p.x_far, p.core]
    )

    def keep_total(v):
        total[...] = v

    def write_output(v):
        output[...] = (middle[...] + v).astype(BF)

    def side(ref, far, near, last, own):
        def mine(d, h):
            start = lax.rem(p.z + d, 4) * 256
            return ref.at[:, pl.ds(pl.multiple_of(start + 128 * h, 128), 128)]

        spans = (pl.ds(0, 128), pl.ds(128, 128))
        yield from ring_reduce(
            w,
            p.z_up,
            p.z_dn,
            mine,
            far.at[0],
            far.at[1],
            lambda h: near.at[0, :, spans[h]],
            lambda h: near.at[1, :, spans[h]],
        )
        block = pl.ds(pl.multiple_of(p.z * 256, 256), 256)

        def summed(e):
            return (
                ref[e, block].astype(F32) + near[0, e].astype(F32) + near[1, e].astype(F32)
            )

        near[0, 1 - p.xl] = summed(1 - p.xl).astype(BF)
        copy = w.send(near.at[0, 1 - p.xl], last, p.x_near)
        yield
        mine_now = summed(p.xl)
        copy.wait_recv()
        own[...] = (mine_now + last[...].astype(F32)).astype(BF)

    def down():
        copy = w.send(dd.at[1 - p.xl], dx, p.x_near)
        yield
        copy.wait_recv()
        dmine[...] = add_low(dd[p.xl], dx[...])

        def mine(d, h):
            start = lax.rem(p.z + d, 4) * 128
            return dmine.at[pl.ds(pl.multiple_of(start + 64 * h, 64), 64)]

        spans = (pl.ds(0, 64), pl.ds(64, 64))
        yield from ring_reduce(
            w,
            p.z_up,
            p.z_dn,
            mine,
            dfar.at[0],
            dfar.at[1],
            lambda h: dnear.at[0, spans[h]],
            lambda h: dnear.at[1, spans[h]],
        )
        block = dmine[pl.ds(pl.multiple_of(p.z * 128, 128), 128)].astype(F32)
        own_d[...] = (block + dnear[0].astype(F32) + dnear[1].astype(F32)).astype(BF)

    def tail():
        yield from reduce16(w, p, grads, go, ga, gf, gn, gl, keep_total)
        yield
        m = middle[...]
        gm = total[...] * gain[...]
        r = lax.rsqrt(jnp.mean(m * m, axis=-1, keepdims=True) + 1e-5)
        inner = jnp.mean(gm * m, axis=-1, keepdims=True)
        gmid = cot[...].astype(F32) + r * gm - m * (r * r * r * inner)
        grad_middle[...] = gmid
        grad_gain[...] = jnp.broadcast_to(
            jnp.sum(total[...] * (m * r), axis=0, keepdims=True), (8, 1024)
        )
        branch[...] = gmid.astype(BF)
        for t in range(4):
            cols = slice(256 * t, 256 * t + 256)
            back[:, cols] = dot_nt(branch[...], wos[cols, :]).astype(BF)
        place = pl.ds(pl.multiple_of(p.c * 128, 128), 128)
        keep = pltpu.make_async_copy(back.at[:, place], dctx.at[p.c], local)
        keep.start()
        arrivals = []
        for i in range(1, 8):
            to = lax.rem(p.c + i, 8)
            block = pl.ds(pl.multiple_of(to * 128, 128), 128)
            arrivals.append(w.send(back.at[:, block], dctx.at[p.c], (to, p.f)))
        yield
        for t in range(16):
            rows = slice(64 * t, 64 * t + 64)
            if t % 2 == 0:
                two = dot_tn(ctx_rows[:, 64 * t : 64 * t + 128], branch[...]).astype(BF)
                grad_out[t] = two[0:64]
                grad_out[t + 1] = two[64:128]
        for copy in arrivals:
            copy.wait_recv()
        keep.wait()

    run_all(
        [
            tail(),
            side(dg, gfar, gnear, gx, own_g),
            side(du, ufar, unear, ux, own_u),
            down(),
            reduce16(w, p, outs, oo, oa, of, on, ol, write_output),
        ]
    )
    w.done()


def return_reduce(grads, outs, dg, du, dd, middle, cot, wos, gain, ctx_rows):
    def side():
        return [
            pltpu.VMEM((2, 2, 128, 512), BF),
            pltpu.VMEM((2, 2, 256, 512), BF),
            pltpu.VMEM((256, 512), BF),
        ]

    return pl.pallas_call(
        return_kernel,
        name="return_reduce",
        out_shape=(
            shaped((128, 1024), BF),
            shaped((128, 1024), F32),
            shaped((8, 1024), F32),
            shaped((8, 128, 128), BF),
            shaped((16, 64, 1024), BF),
            shaped((256, 512), BF),
            shaped((256, 512), BF),
            shaped((128, 1024), BF),
        ),
        in_specs=[VM] * 10,
        out_specs=(VM, VM, VM, ANY, VM, VM, VM, VM),
        scratch_shapes=reduce16_scratch(128, 1024)
        + reduce16_scratch(128, 1024)
        + side()
        + side()
        + [
            pltpu.VMEM((512, 1024), BF),
            pltpu.VMEM((512, 1024), BF),
            pltpu.VMEM((2, 64, 1024), BF),
            pltpu.VMEM((2, 128, 1024), BF),
            pltpu.VMEM((128, 1024), F32),
            pltpu.VMEM((128, 1024), BF),
            pltpu.VMEM((128, 1024), BF),
            pltpu.SemaphoreType.DMA((96,)),
            pltpu.SemaphoreType.DMA((96,)),
            pltpu.SemaphoreType.DMA,
        ],
        compiler_params=remote_params(3),
    )(grads, outs, dg, du, dd, middle, cot, wos, gain, ctx_rows)


def backward_kernel(
    dctx, ctx_full, qx, kx, vx, raw, normed, xs, wps, qk_gain, trig,
    partial, grad_w, grad_norm, grad_gains,
    gx, dq, dk, dv, dqkv,
):
    low = lanes((128, 128)) < 64

    def prepare(b, carry):
        d = dctx[b].astype(F32)
        prod = d * ctx_full[b]
        left = jnp.sum(jnp.where(low, prod, 0.0), axis=-1, keepdims=True)
        right = jnp.sum(jnp.where(low, 0.0, prod), axis=-1, keepdims=True)
        gx[0, b] = jnp.where(low, d, columns3(-left, 64, (128, 128))).astype(BF)
        gx[1, b] = jnp.where(
            low, pltpu.roll(d, 64, 1), columns3(-right, 64, (128, 128))
        ).astype(BF)
        return carry

    lax.fori_loop(0, 8, prepare, 0)
    dq[...] = jnp.zeros(dq.shape, F32)

    def block(b, carry):
        k = kx[b]
        v = vx[b]
        grad_k = jnp.zeros((128, 128), F32)
        grad_v = jnp.zeros((128, 128), F32)
        for h in range(2):
            q_all = qx[h].reshape(1024, 128)
            g_all = gx[h].reshape(1024, 128)
            pt = jnp.exp(dot_nt(k, q_all))
            dst = (pt * dot_nt(v, g_all)).astype(BF)
            grad_v = grad_v + dot(pt.astype(BF), g_all)
            grad_k = grad_k + dot(dst, q_all)
            dq[h] += dot_tn(dst, k)
        dk[b] = grad_k
        dv[b] = grad_v
        return carry

    lax.fori_loop(0, 8, block, 0)

    weights = wps[:, 0:64, :].reshape(1024, 256)

    def finish(b, carry):
        norm_sum, q_sum, k_sum = carry
        rows = pl.ds(pl.multiple_of(b * 128, 128), 128)
        cos, sin = trig[0, b], trig[1, b]
        gq = jnp.where(low, dq[0, rows, :], pltpu.roll(dq[1, rows, :], 64, 1)) * 0.125
        gq = gq.astype(BF).astype(F32)
        gkv = jnp.where(low, dk[b], pltpu.roll(dv[b], 64, 1)).astype(BF).astype(F32)
        gq = gq * cos - spin(gq) * sin
        gkv_rot = gkv * cos - spin(gkv) * sin
        q, kv = raw[b, :, 0:128], raw[b, :, 128:256]
        rq = lax.rsqrt(head_sums(q * q) * (1.0 / 64) + 1e-6)
        rk = lax.rsqrt(head_sums(kv * kv) * (1.0 / 64) + 1e-6)
        q_sum = q_sum + jnp.sum(gq * q * rq, axis=0, keepdims=True)
        k_sum = k_sum + jnp.sum(gkv_rot * kv * rk, axis=0, keepdims=True)
        gq = gq * qk_gain[0:1]
        gk = gkv_rot * qk_gain[1:2]
        gq = rq * gq - q * (rq * rq * rq) * (head_sums(gq * q) * (1.0 / 64))
        gk = rk * gk - kv * (rk * rk * rk) * (head_sums(gk * kv) * (1.0 / 64))
        gkv = jnp.where(low, gk, gkv)
        dqkv[rows, 0:128] = gq.astype(BF)
        dqkv[rows, 128:256] = gkv.astype(BF)
        gn = dot_nt(dqkv[rows, :], weights)
        partial[b] = gn.astype(BF)
        x = xs[b].astype(F32)
        r = lax.rsqrt(jnp.mean(x * x, axis=-1, keepdims=True) + 1e-5)
        norm_sum = norm_sum + jnp.sum(gn * (x * r), axis=0, keepdims=True)
        return norm_sum, q_sum, k_sum

    zero = jnp.zeros((1, 128), F32)
    norm_sum, q_sum, k_sum = lax.fori_loop(
        0, 8, finish, (jnp.zeros((1, 1024), F32), zero, zero)
    )
    grad_norm[...] = jnp.broadcast_to(norm_sum, (8, 1024))
    low1 = lanes((1, 128)) < 64
    q_sum = q_sum + pltpu.roll(q_sum, 64, 1)
    grad_gains[...] = jnp.broadcast_to(jnp.where(low1, q_sum, pltpu.roll(k_sum, 64, 1)), (8, 128))
    for t in range(4):
        part = dot_tn(normed[:, :, 256 * t : 256 * t + 256].reshape(1024, 256), dqkv[...])
        grad_w[4 * t : 4 * t + 4] = part.astype(BF).reshape(4, 64, 256)


def attend_back(dctx, ctx_full, qx, kx, vx, raw, normed, xs, wps, qk_gain, trig):
    return pl.pallas_call(
        backward_kernel,
        name="attend_back",
        out_shape=(
            shaped((8, 128, 1024), BF),
            shaped((16, 64, 256), BF),
            shaped((8, 1024), F32),
            shaped((8, 128), F32),
        ),
        in_specs=[VM] * 11,
        out_specs=(VM,) * 4,
        scratch_shapes=[
            pltpu.VMEM((2, 8, 128, 128), BF),
            pltpu.VMEM((2, 1024, 128), F32),
            pltpu.VMEM((8, 128, 128), F32),
            pltpu.VMEM((8, 128, 128), F32),
            pltpu.VMEM((1024, 256), BF),
        ],
        compiler_params=local_params(),
    )(dctx, ctx_full, qx, kx, vx, raw, normed, xs, wps, qk_gain, trig)


def last_kernel(
    partial, grad_w, grad_out, small, own_g, own_u, own_d, x, grad_middle, gain,
    input_grad, w_all, out_all, small_sum, dg, du, dd,
    wo_, wa, wf, wn, wl, oo, oa, of, on, ol,
    xr, acc, zfar, znear, w_own, out_own, out_parts, out_mine, ctx_small, mid_small, fsdp_small,
    total, ssem, rsem, local,
):
    p = Place()
    w = Wire(ssem, rsem)
    greet(
        [p.ctx_peer(i) for i in range(1, 8)]
        + [p.fsdp_peer(i) for i in range(1, 16)]
    )

    def tokens():
        def mine(d, h):
            start = lax.rem(p.z + d, 4) * 2
            return partial.at[pl.ds(start, 2), pl.ds(64 * h, 64)]

        spans = (pl.ds(0, 64), pl.ds(64, 64))
        yield from ring_reduce(
            w,
            p.z_up,
            p.z_dn,
            mine,
            zfar.at[0],
            zfar.at[1],
            lambda h: znear.at[0, :, spans[h]],
            lambda h: znear.at[1, :, spans[h]],
        )

        def summed(e):
            return (
                partial[2 * p.z + e].astype(F32) + znear[0, e].astype(F32) + znear[1, e].astype(F32)
            )

        acc[...] = summed(1 - p.xl).astype(BF)
        copy = w.send(acc, xr, p.x_near)
        yield
        total[...] = summed(p.xl)
        copy.wait_recv()
        gy = (total[...] + xr[...].astype(F32)) * gain[...]
        v = x[...].astype(F32)
        r = lax.rsqrt(jnp.mean(v * v, axis=-1, keepdims=True) + 1e-5)
        inner = jnp.mean(gy * v, axis=-1, keepdims=True)
        input_grad[...] = grad_middle[...] + r * gy - v * (r * r * r * inner)

    def projections():
        def finish(v):
            w_own[...] = v.astype(BF)

        yield from reduce16(w, p, grad_w, wo_, wa, wf, wn, wl, finish)
        yield
        yield from gather8(w, p, w_own, w_all, 32, local.at[0])

    def out_weight():
        def finish(v):
            for i in range(8):
                out_own[i] = v[:, 128 * i : 128 * i + 128].astype(BF)

        yield from reduce16(w, p, grad_out, oo, oa, of, on, ol, finish)
        arrivals = []
        for i in range(1, 8):
            to = lax.rem(p.c + i, 8)
            arrivals.append(w.send(out_own.at[to], out_parts.at[i - 1], (to, p.f)))
        yield
        sums = out_own[p.c].astype(F32)
        for i, copy in enumerate(arrivals):
            copy.wait_recv()
            sums = sums + out_parts[i].astype(F32)
        out_mine[...] = sums.astype(BF)
        yield
        yield from gather8(w, p, out_mine, out_all, 32, local.at[1])

    def vectors():
        first = [
            w.send(small, ctx_small.at[i - 1], p.ctx_peer(i)) for i in range(1, 8)
        ]
        yield
        sums = small[...]
        for i, copy in enumerate(first):
            copy.wait_recv()
            sums = sums + ctx_small[i]
        mid_small[...] = sums
        second = [
            w.send(mid_small, fsdp_small.at[p.f], p.fsdp_peer(i)) for i in range(1, 16)
        ]
        fsdp_small[p.f] = sums
        yield
        for copy in second:
            copy.wait_recv()
        sums = fsdp_small[0]
        for i in range(1, 16):
            sums = sums + fsdp_small[i]
        small_sum[...] = sums

    def side(own, out, sem):
        def block(dz, e=None):
            rows = pl.ds(pl.multiple_of(lax.rem(p.z + dz, 4) * 256, 256), 256)
            return out.at[:, rows] if e is None else out.at[e, rows]

        def half(dz, h):
            start = lax.rem(p.z + dz, 4) * 256 + 128 * h
            return out.at[:, pl.ds(pl.multiple_of(start, 128), 128)]

        keep = pltpu.make_async_copy(own, block(0, p.xl), sem)
        keep.start()
        a = w.send(own, block(0, p.xl), p.x_near)
        yield
        keep.wait()
        a.wait_recv()
        up = w.send(block(0), block(0), p.z_up)
        down = w.send(block(0), block(0), p.z_dn)
        yield
        up.wait_recv()
        c = w.send(half(3, 0), half(3, 0), p.z_up)
        down.wait_recv()
        d = w.send(half(1, 1), half(1, 1), p.z_dn)
        yield
        c.wait_recv()
        d.wait_recv()

    def downs():
        def block(dz):
            return dd.at[p.xl, pl.ds(pl.multiple_of(lax.rem(p.z + dz, 4) * 128, 128), 128)]

        def half(dz, h):
            start = lax.rem(p.z + dz, 4) * 128 + 64 * h
            return dd.at[p.xl, pl.ds(pl.multiple_of(start, 64), 64)]

        keep = pltpu.make_async_copy(own_d, block(0), local.at[4])
        keep.start()
        up = w.send(own_d, block(0), p.z_up)
        down = w.send(own_d, block(0), p.z_dn)
        near = [w.send(own_d, block(0), p.x_near)]
        yield
        up.wait_recv()
        c = w.send(half(3, 0), half(3, 0), p.z_up)
        near.append(w.send(block(3), block(3), p.x_near))
        down.wait_recv()
        d = w.send(half(1, 1), half(1, 1), p.z_dn)
        near.append(w.send(block(1), block(1), p.x_near))
        yield
        c.wait_recv()
        d.wait_recv()
        near.append(w.send(block(2), block(2), p.x_near))
        yield
        for copy in near:
            copy.wait_recv()
        keep.wait()

    run_all(
        [
            tokens(),
            vectors(),
            projections(),
            out_weight(),
            side(own_g, dg, local.at[2]),
            side(own_u, du, local.at[3]),
            downs(),
        ]
    )
    w.done()


def last_reduce(partial, grad_w, grad_out, small, own_g, own_u, own_d, x, grad_middle, gain):
    return pl.pallas_call(
        last_kernel,
        name="last_reduce",
        out_shape=(
            shaped((128, 1024), F32),
            shaped((8, 64, 256), BF),
            shaped((8, 64, 128), BF),
            shaped(small.shape, F32),
            shaped((2, 1024, 512), BF),
            shaped((2, 1024, 512), BF),
            shaped((2, 512, 1024), BF),
        ),
        in_specs=[VM] * 10,
        out_specs=(VM, ANY, ANY, VM, ANY, ANY, ANY),
        scratch_shapes=reduce16_scratch(64, 256)
        + reduce16_scratch(64, 1024)
        + [
            pltpu.VMEM((128, 1024), BF),
            pltpu.VMEM((128, 1024), BF),
            pltpu.VMEM((2, 2, 64, 1024), BF),
            pltpu.VMEM((2, 2, 128, 1024), BF),
            pltpu.VMEM((64, 256), BF),
            pltpu.VMEM((8, 64, 128), BF),
            pltpu.VMEM((7, 64, 128), BF),
            pltpu.VMEM((64, 128), BF),
            pltpu.VMEM((7,) + small.shape, F32),
            pltpu.VMEM(small.shape, F32),
            pltpu.VMEM((16,) + small.shape, F32),
            pltpu.VMEM((128, 1024), F32),
            pltpu.SemaphoreType.DMA((128,)),
            pltpu.SemaphoreType.DMA((128,)),
            pltpu.SemaphoreType.DMA((5,)),
        ],
        compiler_params=remote_params(4),
    )(partial, grad_w, grad_out, small, own_g, own_u, own_d, x, grad_middle, gain)


def trig_tables():
    index = np.arange(1024)
    stored = index // 64
    natural = np.where(stored % 2 == 0, stored // 2, 15 - stored // 2)
    pos = (natural * 64 + index % 64).astype(np.float32)
    freq = (10000.0 ** (-np.arange(32) * 2.0 / 64)).astype(np.float32)
    angle = (pos[:, None] * freq[None, :]).astype(np.float64)
    cos, sin = np.cos(angle), np.sin(angle)
    cos = np.concatenate([cos] * 4, axis=1)
    sin = np.concatenate([-sin, sin, -sin, sin], axis=1)
    return np.stack([cos, sin]).astype(np.float32).reshape(2, 8, 128, 128)


def on_device(
    inputs, segments, routes, gate_weights, cotangent, norm_in, norm_mid, q_gain, k_gain,
    w_query, w_key, w_value, w_out, w_gate, w_up, w_down,
):
    c = lax.axis_index("ctx")
    f = lax.axis_index("fsdp")
    x, cot = inputs[0], cotangent[0]
    trig = jnp.asarray(trig_tables())
    wp = jnp.concatenate(
        [
            lax.dynamic_slice(w_query, (0, 128 * c), (64, 128)),
            lax.dynamic_slice(w_key, (0, 64 * c), (64, 64)),
            lax.dynamic_slice(w_value, (0, 64 * c), (64, 64)),
        ],
        axis=1,
    )
    gains = jnp.pad(jnp.concatenate([norm_in, norm_mid])[None], ((0, 15), (0, 128)))
    wp = jnp.concatenate([wp, gains], axis=0)
    seg = jnp.broadcast_to(segments, (8, 128))
    expert_ids = jnp.arange(EXPERTS, dtype=jnp.int32)
    g = jnp.sum(
        jnp.where(
            routes[0].T[None, :, :] == expert_ids[:, None, None], gate_weights[0].T[None], 0.0
        ),
        axis=1,
    )
    ones = jnp.ones((64,), F32)
    qk_gain = jnp.stack(
        [
            jnp.concatenate([q_gain, q_gain]).astype(F32),
            jnp.concatenate([k_gain.astype(F32), ones]),
        ]
    )
    xs, segs, wps, wos, gs, cots = first_gather(x, seg, wp, w_out, g, cot)
    gain_in = wps[:, 64, 0:64].reshape(1, 1024).astype(F32)
    gain_mid = wps[:, 64, 64:128].reshape(1, 1024).astype(F32)
    wo_full = wos.reshape(1024, 1024)
    normed, raw, qx, kx, vx, ctx_full, ctx_low = attend(xs, segs, wps, gain_in, qk_gain, trig)
    middle, ctx_rows, mids = middle_gather(ctx_low, x, wo_full, gain_mid)
    outs, grads, dg, du, dd = experts(gs, mids, cots, w_gate, w_up, w_down)
    output, grad_middle, grad_gain_mid, dctx, grad_out, own_g, own_u, own_d = return_reduce(
        grads, outs, dg, du, dd, middle, cot, wo_full, gain_mid, ctx_rows
    )
    partial, grad_w, grad_gain_in, grad_gains = attend_back(
        dctx, ctx_full, qx, kx, vx, raw, normed, xs, wps, qk_gain, trig
    )
    small = jnp.concatenate(
        [
            grad_gain_in[0].reshape(8, 128),
            grad_gain_mid[0].reshape(8, 128),
            grad_gains,
        ]
    )
    input_grad, w_all, out_all, small_sum, dg, du, dd = last_reduce(
        partial, grad_w, grad_out, small, own_g, own_u, own_d, x, grad_middle, gain_in
    )
    grad_wq = w_all[:, :, 0:128].transpose(1, 0, 2).reshape(64, 1024).astype(F32)
    grad_wk = w_all[:, :, 128:192].transpose(1, 0, 2).reshape(64, 512).astype(F32)
    grad_wv = w_all[:, :, 192:256].transpose(1, 0, 2).reshape(64, 512).astype(F32)
    grad_wo = out_all.transpose(1, 0, 2).reshape(64, 1024).astype(F32)
    grad_norm_in = lax.dynamic_slice(small_sum[0:8].reshape(1024), (64 * f,), (64,))
    grad_norm_mid = lax.dynamic_slice(small_sum[8:16].reshape(1024), (64 * f,), (64,))
    return (
        output[None],
        input_grad[None],
        grad_norm_in,
        grad_norm_mid,
        small_sum[16, 0:64],
        small_sum[16, 64:128],
        grad_wq,
        grad_wk,
        grad_wv,
        grad_wo,
        dg.astype(F32),
        du.astype(F32),
        dd.astype(F32),
    )


def solution(mesh):
    rows = P("fsdp", "ctx", None)
    in_specs = (
        rows,
        P("fsdp", "ctx"),
        rows,
        rows,
        rows,
        P("fsdp"),
        P("fsdp"),
        P(),
        P(),
        P("fsdp", None),
        P("fsdp", None),
        P("fsdp", None),
        P("fsdp", None),
        P("fsdp", None, None),
        P("fsdp", None, None),
        P("fsdp", None, None),
    )
    out_specs = (
        rows,
        rows,
        P("fsdp"),
        P("fsdp"),
        P(),
        P(),
        P("fsdp", None),
        P("fsdp", None),
        P("fsdp", None),
        P("fsdp", None),
        P("fsdp", None, None),
        P("fsdp", None, None),
        P("fsdp", None, None),
    )
    return jax.shard_map(
        on_device, mesh=mesh, in_specs=in_specs, out_specs=out_specs, check_vma=False
    )
```

time: 1190 us -> 351 us (0.29)
  waiting for transfers between devices: 707 us -> 0 us
  Pallas kernels: 0 us -> 319 us
  blocking collectives: 205 us -> 0 us
  matrix products: 114 us -> 0 us
  other arithmetic: 63.6 us -> 18.5 us
  local copies, waits for them, and re-layouts: 53.2 us -> 12.2 us
  starting transfers between devices: 19.4 us -> 0 us
  between operations: 16.4 us -> 0.75 us
    pallas_call x0 -> x7, Pallas kernels: none -> 319 us  [the longest x1 88.2 us: last_reduce(): pl.pallas_call(last_kernel, name='last_reduce', out_shape=(shaped((128, 1...]
    reduce_scatter x4 -> x0, waiting for transfers between devices: 274 us -> none  [the longest x1 74.8 us: on_device(): lax.psum_scatter(grad_wq.astype(jnp.bfloat16), 'fsdp', scatter_dimension=...]
    psum x1 -> x0, waiting for transfers between devices: 160 us -> none  [on_device(): lax.psum(part_wq.astype(jnp.bfloat16), 'ctx').astype(jnp.float32)]
    dot_general x79 -> x0, matrix products: 114 us -> none  [the longest x16 21.3 us: masked_scores(): jnp.einsum('qgd,kd->gqk', query_head, key_head, preferred_element_type=jn...]
    all_gather x6 -> x0, waiting for transfers between devices: 111 us -> none  [the longest x1 42.2 us: on_device(): lax.all_gather(w_key, 'fsdp', axis=0, tiled=True)]
    all_to_all x4 -> x0, waiting for transfers between devices: 88.4 us -> none  [the longest x1 31.4 us: on_device(): lax.all_to_all(slots_in.reshape(n_fsdp, own_experts, CAP, width), 'fsdp',...]
    psum x2 -> x0, blocking collectives: 86 us -> none  [the longest x1 65.4 us: on_device(): lax.psum((grad_q_part, grad_k_part), ('ctx', 'fsdp'))]
    unnamed x15 -> x0, waiting for transfers between devices: 73.6 us -> none
  transfers between devices with their start and end apart: 17 -> 0, of which waited for: 15 -> 0; matrix products, arithmetic and copies ran while one was open for 11% -> 0% of each run, Pallas kernels for 0% -> 0%
where the time goes in v1:
time: 351 us
  Pallas kernels  319 us (91%)
  other arithmetic  18.5 us (5%)
  local copies, waits for them, and re-layouts  12.2 us (3%)
    pallas_call x1, Pallas kernels, last_reduce(): pl.pallas_call(last_kernel, name='last_reduce', out_shape=(shaped((128, 1...  88.2 us
    pallas_call x1, Pallas kernels, return_reduce(): pl.pallas_call(return_kernel, name='return_reduce', out_shape=(shaped((12...  75.6 us
    pallas_call x1, Pallas kernels, first_gather(): pl.pallas_call(first_kernel, name='first_gather', out_shape=(shaped((8,)...  45.1 us
    pallas_call x1, Pallas kernels, experts(): pl.pallas_call(expert_kernel, name='experts', out_shape=(shaped((16, 128,...  41.3 us
    pallas_call x1, Pallas kernels, middle_gather(): pl.pallas_call(middle_kernel, name='middle_gather', out_shape=(shaped((12...  34.1 us
    pallas_call x1, Pallas kernels, attend_back(): pl.pallas_call(backward_kernel, name='attend_back', out_shape=(shaped((8,...  20.2 us
    pallas_call x1, Pallas kernels, attend(): pl.pallas_call(attend_kernel, name='attend', out_shape=(shaped((8, 128, 1...  14.8 us

profile of v1, /device:TPU:0, one launch (start us, length us, event | category | flops | bytes accessed | tf_op | source)
XLA Modules:
  0.0 350.8 jit_solution(11257681244710751303)
XLA Ops:
  0.6 0.0 copy-start
  0.7 0.8 maximum_bitcast_fusion
  1.5 0.7 pad_bitcast_fusion
  2.1 1.4 maximum_convert_fusion.qk_gain
  3.5 1.2 broadcast_in_dim.33.seg
  4.7 0.0 copy-done
  4.7 1.4 select_reduce_fusion.g
  6.1 0.8 constant_dynamic-slice_fusion
  6.9 0.7 fusion.1.wp
  7.6 45.1 %first_gather.1 = (bf16[8,128,1024]{2,1,0:T(8,128)(2,1)}, s32[8,8,128]{2,1,0:T(8,128)}, bf16[16,80,256]{2,1,0:T(8,128)(2,1)}, bf16[16,64,1024]{2,1,0:T(8,128)(2,...) custom-call(bf16[128,1024]{1,0:T(8,128)(2,1)} %bitcast.45, s32[8,128]{1,0:T(8,128)} %broadcast_in_dim.33.seg, ...), custom_call_target="tpu_custom_call" | custom-call | tf_op jit(solution)/shard_map/first_gather/pallas_call | solution.py:272
  52.7 0.9 convert_reduce_fusion
  53.6 0.7 reshape.110.gain
  54.3 0.7 reshape.109.gain
  55.0 14.8 %attend.1 = (bf16[8,128,1024]{2,1,0:T(8,128)(2,1)}, f32[8,128,256]{2,1,0:T(8,128)}, bf16[2,8,128,128]{3,2,1,0:T(8,128)(2,1)}, bf16[8,128,128]{2,1,0:T(8,128)(2,1...) custom-call(bf16[8,128,1024]{2,1,0:T(8,128)(2,1)} %get-tuple-element.54.xs, ...), custom_call_target="tpu_custom_call" | custom-call | tf_op jit(solution)/shard_map/attend/pallas_call | solution.py:381
  69.8 34.1 %middle_gather.1 = (f32[128,1024]{1,0:T(8,128)}, bf16[128,1024]{1,0:T(8,128)(2,1)}, bf16[16,128,1024]{2,1,0:T(8,128)(2,1)}) custom-call(bf16[8,128,128]{2,1,0:T(8,128)(2,1)} %get-tuple-element.57.ctx, bf16[128,1024]{1,0:T(8,128)(2,1)} %bitcast.46, bf16[1024,1024]{1,0:T(8,128)(2,1)} %bitcast.43, f32[1,1024]{1,0:T(1,128)} %reshape.110.gain), custom_call_target="tpu_custom_call" | custom-call | tf_op jit(solution)/shard_map/middle_gather/pallas_call | solution.py:426
  103.9 41.3 %experts.1 = (bf16[16,128,1024]{2,1,0:T(8,128)(2,1)}, bf16[16,128,1024]{2,1,0:T(8,128)(2,1)}, bf16[2,1024,512]{2,1,0:T(8,128)(2,1)}, bf16[2,1024,512]{2,1,0:T(8,128)(2,1)}, bf16[2,512,1024]{2,1,0:T(8,128)(2,1)}) custom-call(f32[16,32,128]{2,1,0:T(8,128)} %get-tuple-element.53.gs, bf16[16,128,1024]{2,1,0:T(8,128)(2,1)} %get-tuple-element.59.mids, ...), custom_call_target="tpu_custom_call" | custom-call | tf_op jit(solution)/shard_map/experts/pallas_call | solution.py:523
  145.3 75.6 %return_reduce.1 = (bf16[128,1024]{1,0:T(8,128)(2,1)}, f32[128,1024]{1,0:T(8,128)}, f32[8,1024]{1,0:T(8,128)}, bf16[8,128,128]{2,1,0:T(8,128)(2,1)}, bf16[16,64,...) custom-call(bf16[16,128,1024]{2,1,0:T(8,128)(2,1)} %get-tuple-element.61.gr, ...), custom_call_target="tpu_custom_call" | custom-call | tf_op jit(solution)/shard_map/return_reduce/pallas_call | solution.py:681
  220.8 20.2 %attend_back.1 = (bf16[8,128,1024]{2,1,0:T(8,128)(2,1)}, bf16[16,64,256]{2,1,0:T(8,128)(2,1)}, f32[8,1024]{1,0:T(8,128)}, f32[8,128]{1,0:T(8,128)}) custom-call(bf16[8,128,128]{2,1,0:T(8,128)(2,1)} %get-tuple-element.69.dctx, f32[8,128,128]{2,1,0:T(8,128)} %get-tuple-element.70.ctx_full, bf16[2,8,128,128]{3,2,1,0:T(8,128)(2,1)} %get-tuple-element.71.qx, ...), custom_call_target="tpu_custom_call" | custom-call | tf_op jit(solution)/shard_map/attend_back/pallas_call | solution.py:800
  241.0 0.8 slice.35
  241.8 0.8 slice.36
  242.5 1.3 pad_maximum_fusion.small
  243.8 88.2 %last_reduce.1 = (f32[128,1024]{1,0:T(8,128)}, bf16[8,64,256]{2,1,0:T(8,128)(2,1)}, bf16[8,64,128]{2,1,0:T(8,128)(2,1)}, f32[24,128]{1,0:T(8,128)}, bf16[2,1024,...) custom-call(bf16[8,128,1024]{2,1,0:T(8,128)(2,1)} %get-tuple-element.76.partial, ...), custom_call_target="tpu_custom_call" | custom-call | tf_op jit(solution)/shard_map/last_reduce/pallas_call | solution.py:988
  332.0 0.0 copy-start.4
  332.1 1.4 slice_bitcast_fusion.2
  333.5 0.7 slice_bitcast_fusion
  334.2 0.6 dynamic_slice.19
  334.7 0.6 dynamic_slice.18
  335.3 1.6 copy_bitcast_fusion
  337.0 1.6 copy_bitcast_fusion.1
  338.6 1.1 convert_bitcast_fusion.1
  339.7 0.2 copy.36
  339.8 0.8 reshape.113
  340.6 0.2 copy.35
  340.8 0.8 reshape.112
  341.5 0.0 copy-done.4
  341.5 0.0 copy-start.3
  341.5 2.6 convert_element_type.82
  344.1 0.0 copy-done.3
  344.1 0.0 copy-start.2
  344.1 2.6 convert_element_type.83
  346.8 0.0 copy-done.2
  346.8 0.0 copy-start.6
  346.8 0.0 copy-start.5
  346.8 0.0 copy-start.1
  346.8 2.5 convert_element_type.84
  349.3 0.0 copy-done.6
  349.3 0.7 copy.44
  350.0 0.0 copy-done.5
  350.0 0.8 copy.45
  350.8 0.0 copy-done.1
  (1 shorter events, 0.0 us)
Async XLA Ops:
  0.6 4.1 %copy-start = (bf16[64,1024]{1,0:T(8,128)(2,1)S(1)}, bf16[64,1024]{1,0:T(8,128)(2,1)}, u32[]{:S(2)}) copy-start(bf16[64,1024]{1,0:T(8,128)(2,1)} %param.26) | copy-start | bytes 393220
  332.0 9.5 %copy-start.4 = (bf16[2,1024,512]{2,1,0:T(8,128)(2,1)S(1)}, bf16[2,1024,512]{2,1,0:T(8,128)(2,1)}, u32[]{:S(2)}) copy-start(bf16[2,1024,512]{2,1,0:T(8,128)(2,1)} %get-tuple-element.90) | copy-start | bytes 6291460
  341.5 2.6 copy-start.3
  344.1 2.6 copy-start.2
  346.8 2.5 copy-start.6
  346.8 3.2 copy-start.5
  346.8 4.0 %copy-start.1 = (bf16[64,1024]{1,0:T(8,128)(2,1)S(1)}, bf16[64,1024]{1,0:T(8,128)(2,1)}, u32[]{:S(2)}) copy-start(bf16[64,1024]{1,0:T(8,128)(2,1)} %param.26) | copy-start | bytes 393220

commit v2 on v1

v2 whole, which is shorter than its diff:
```python
from types import SimpleNamespace

import jax
import jax.numpy as jnp
import numpy as np
from jax import lax
from jax.experimental import pallas as pl
from jax.experimental.pallas import tpu as pltpu
from jax.sharding import PartitionSpec as P

F32 = jnp.float32
BF = jnp.bfloat16
MESH = pl.DeviceIdType.MESH
EXPERTS = 32
CAP = 40
NEG = 128.0
ANY = pl.BlockSpec(memory_space=pl.ANY)
VM = pl.BlockSpec(memory_space=pltpu.VMEM)
LIMIT = 62 << 20


def dot(a, b):
    return jnp.dot(a, b, preferred_element_type=F32)


def dot_nt(a, b):
    return lax.dot_general(a, b, (((1,), (1,)), ((), ())), preferred_element_type=F32)


def dot_tn(a, b):
    return lax.dot_general(a, b, (((0,), (0,)), ((), ())), preferred_element_type=F32)


def add_low(a, b):
    return (a.astype(F32) + b.astype(F32)).astype(BF)


class Place:
    def __init__(self):
        c = lax.axis_index("ctx")
        f = lax.axis_index("fsdp")
        self.c, self.f = c, f
        self.z, self.xl = c // 2, lax.rem(c, 2)
        self.y, self.xh, self.k = f // 4, lax.rem(f // 2, 2), lax.rem(f, 2)
        self.cx = c + 1 - 2 * self.xl
        self.fx = f + 2 - 4 * self.xh
        self.z_up = (lax.rem(c + 2, 8), f)
        self.z_dn = (lax.rem(c + 6, 8), f)
        self.x_near = (self.cx, f)
        self.y_up = (c, lax.rem(f + 4, 16))
        self.y_dn = (c, lax.rem(f + 12, 16))
        self.x_far = (c, self.fx)
        self.core = (c, f + 1 - 2 * self.k)

    def ctx_peer(self, i):
        return (lax.rem(self.c + i, 8), self.f)

    def fsdp_peer(self, i):
        return (self.c, lax.rem(self.f + i, 16))


class Wire:
    def __init__(self, ssem, rsem):
        self.ssem, self.rsem = ssem, rsem
        self.started = []

    def send(self, src, dst, device):
        n = len(self.started)
        copy = pltpu.make_async_remote_copy(
            src_ref=src,
            dst_ref=dst,
            send_sem=self.ssem.at[n],
            recv_sem=self.rsem.at[n],
            device_id=device,
            device_id_type=MESH,
        )
        copy.start()
        self.started.append(copy)
        return copy

    def done(self):
        for copy in self.started:
            copy.wait_send()


def greet(devices):
    barrier = pltpu.get_barrier_semaphore()
    for device in devices:
        pl.semaphore_signal(barrier, inc=1, device_id=device, device_id_type=MESH)
    return lambda: pl.semaphore_wait(barrier, len(devices))


class Fetch:
    def __init__(self, sem):
        self.sem, self.n, self.live = sem, 0, {}

    def go(self, name, src, dst):
        copy = pltpu.make_async_copy(src, dst, self.sem.at[self.n])
        copy.start()
        self.n += 1
        self.live.setdefault(name, []).append(copy)

    def need(self, *names):
        for name in names:
            for copy in self.live.pop(name, []):
                copy.wait()


def run_all(steps):
    steps = list(steps)
    while steps:
        alive = []
        for step in steps:
            try:
                next(step)
                alive.append(step)
            except StopIteration:
                pass
        steps = alive


def gather16(w, p, own, out, half, local):
    f, fx = p.f, p.fx
    keep = pltpu.make_async_copy(own, out.at[f], local)
    keep.start()
    from_x = w.send(own, out.at[f], p.x_far)
    rings = [(w.send(own, out.at[f], p.y_up), w.send(own, out.at[f], p.y_dn), f)]
    cores = [w.send(own, out.at[f], p.core)]
    yield
    from_x.wait_recv()
    rings.append((w.send(out.at[fx], out.at[fx], p.y_up), w.send(out.at[fx], out.at[fx], p.y_dn), fx))
    cores.append(w.send(out.at[fx], out.at[fx], p.core))
    yield
    halves = []
    for up, down, slot in rings:
        up.wait_recv()
        low = lax.rem(slot + 12, 16)
        part = out.at[low, pl.ds(0, half)]
        halves.append(w.send(part, part, p.y_up))
        cores.append(w.send(out.at[low], out.at[low], p.core))
        down.wait_recv()
        high = lax.rem(slot + 4, 16)
        part = out.at[high, pl.ds(half, own.shape[0] - half)]
        halves.append(w.send(part, part, p.y_dn))
        cores.append(w.send(out.at[high], out.at[high], p.core))
        yield
    for i, slot in ((0, f), (2, fx)):
        halves[i].wait_recv()
        halves[i + 1].wait_recv()
        far = lax.rem(slot + 8, 16)
        cores.append(w.send(out.at[far], out.at[far], p.core))
        yield
    for copy in cores:
        copy.wait_recv()
    keep.wait()


def gather8(w, p, own, out, half, local):
    c, cx = p.c, p.cx
    keep = pltpu.make_async_copy(own, out.at[c], local)
    keep.start()
    from_x = w.send(own, out.at[c], p.x_near)
    rings = [(w.send(own, out.at[c], p.z_up), w.send(own, out.at[c], p.z_dn), c)]
    yield
    from_x.wait_recv()
    rings.append((w.send(out.at[cx], out.at[cx], p.z_up), w.send(out.at[cx], out.at[cx], p.z_dn), cx))
    yield
    halves = []
    for up, down, slot in rings:
        up.wait_recv()
        part = out.at[lax.rem(slot + 6, 8), pl.ds(0, half)]
        halves.append(w.send(part, part, p.z_up))
        down.wait_recv()
        if half < own.shape[0]:
            part = out.at[lax.rem(slot + 2, 8), pl.ds(half, own.shape[0] - half)]
            halves.append(w.send(part, part, p.z_dn))
        yield
    for copy in halves:
        copy.wait_recv()
    keep.wait()


def ring_reduce(w, up, down, mine, far_up, far_down, near_up, near_down):
    a = w.send(mine(2, 0), far_up, up)
    b = w.send(mine(2, 1), far_down, down)
    yield
    c = w.send(mine(1, 1), near_up(1), up)
    d = w.send(mine(3, 0), near_down(0), down)
    yield
    a.wait_recv()
    far_up[...] = add_low(mine(1, 0)[...], far_up[...])
    e = w.send(far_up, near_up(0), up)
    b.wait_recv()
    far_down[...] = add_low(mine(3, 1)[...], far_down[...])
    g = w.send(far_down, near_down(1), down)
    yield
    for copy in (c, d, e, g):
        copy.wait_recv()


def reduce16(w, p, part, other, far, near, last, finish, produce=None):
    rows = other.shape[2]
    half = rows // 2
    order = (2, 1, 3, 0)
    arrivals = []
    for dy in order:
        for e in (0, 1):
            slot = lax.rem((p.f, p.fx)[e] + 4 * dy, 16)
            if produce is not None:
                produce(slot)
            arrivals.append(w.send(part(slot + 1 - 2 * p.k), other.at[dy, e], p.core))
    yield

    def merge(i, dy):
        for e in (0, 1):
            arrivals[2 * i + e].wait_recv()
            slot = lax.rem((p.f, p.fx)[e] + 4 * dy, 16)
            other[dy, e] = add_low(part(slot)[...], other[dy, e])

    spans = {0: pl.ds(0, half), 1: pl.ds(half, rows - half)}
    ring = ring_reduce(
        w,
        p.y_up,
        p.y_dn,
        lambda dy, h: other.at[dy, :, spans[h]],
        far.at[0],
        far.at[1],
        lambda h: near.at[0, :, spans[h]],
        lambda h: near.at[1, :, spans[h]],
    )
    merge(0, 2)
    next(ring)
    merge(1, 1)
    merge(2, 3)
    next(ring)
    merge(3, 0)
    yield
    next(ring)
    yield
    for _ in ring:
        pass
    other[0, 1] = (
        other[0, 1].astype(F32) + near[0, 1].astype(F32) + near[1, 1].astype(F32)
    ).astype(BF)
    copy = w.send(other.at[0, 1], last, p.x_far)
    yield
    total = other[0, 0].astype(F32) + near[0, 0].astype(F32) + near[1, 0].astype(F32)
    copy.wait_recv()
    finish(total + last[...].astype(F32))


def reduce16_scratch(rows, cols):
    return [
        pltpu.VMEM((4, 2, rows, cols), BF),
        pltpu.VMEM((2, 2, rows // 2, cols), BF),
        pltpu.VMEM((2, 2, rows, cols), BF),
        pltpu.VMEM((rows, cols), BF),
    ]


def remote_params(cid):
    return pltpu.CompilerParams(collective_id=cid, has_side_effects=True, vmem_limit_bytes=LIMIT)


def local_params():
    return pltpu.CompilerParams(vmem_limit_bytes=LIMIT)


def shaped(shape, dtype):
    return jax.ShapeDtypeStruct(shape, dtype)


def first_kernel(x, seg, wp, wo, g, cot, xs, segs, wps, wos, gs, cots, ssem, rsem, local):
    p = Place()
    w = Wire(ssem, rsem)
    greet([p.z_up, p.z_dn, p.x_near, p.y_up, p.y_dn, p.x_far, p.core])()
    run_all(
        [
            gather8(w, p, x, xs, 64, local.at[0]),
            gather8(w, p, seg, segs, 8, local.at[1]),
            gather16(w, p, wp, wps, 48, local.at[2]),
            gather16(w, p, wo, wos, 32, local.at[3]),
            gather16(w, p, g, gs, 16, local.at[4]),
            gather16(w, p, cot, cots, 64, local.at[5]),
        ]
    )
    w.done()


def first_gather(x, seg, wp, wo, g, cot):
    return pl.pallas_call(
        first_kernel,
        name="first_gather",
        out_shape=(
            shaped((8,) + x.shape, BF),
            shaped((8,) + seg.shape, jnp.int32),
            shaped((16,) + wp.shape, BF),
            shaped((16,) + wo.shape, BF),
            shaped((16,) + g.shape, F32),
            shaped((16,) + cot.shape, BF),
        ),
        in_specs=[ANY] * 6,
        out_specs=(ANY,) * 6,
        scratch_shapes=[
            pltpu.SemaphoreType.DMA((96,)),
            pltpu.SemaphoreType.DMA((96,)),
            pltpu.SemaphoreType.DMA((6,)),
        ],
        compiler_params=remote_params(1),
    )(x, seg, wp, wo, g, cot)


def lanes(shape):
    return lax.broadcasted_iota(jnp.int32, shape, len(shape) - 1)


def spin(v):
    first = lax.rem(lanes(v.shape), 64) < 32
    return jnp.where(first, pltpu.roll(v, 96, 1), pltpu.roll(v, 32, 1))


def head_sums(v):
    low = lanes(v.shape) < 64
    left = jnp.sum(jnp.where(low, v, 0.0), axis=-1, keepdims=True)
    right = jnp.sum(jnp.where(low, 0.0, v), axis=-1, keepdims=True)
    return jnp.where(low, left, right)


def split3(v):
    high = v.astype(BF).astype(F32)
    rest = v - high
    mid = rest.astype(BF).astype(F32)
    return high, mid, (rest - mid).astype(BF).astype(F32)


def columns3(v, base, shape):
    where = lanes(shape)
    high, mid, low = split3(v)
    return jnp.where(
        where == base, high, jnp.where(where == base + 1, mid, jnp.where(where == base + 2, low, 0.0))
    )


def attend_kernel(
    xs, segs, wps, gain, qk_gain, trig, normed, raw, qx, kx, vx, ctx_full, ctx_low, q_plain
):
    weights = wps[:, 0:64, :].reshape(1024, 256)
    place = lanes((8, 128))
    docs = lax.broadcasted_iota(jnp.int32, (8, 128), 0)
    spot = jnp.where(place == docs + 64, 1.0, 0.0)
    low = lanes((128, 128)) < 64

    def project(b, carry):
        x = xs[b].astype(F32)
        r = lax.rsqrt(jnp.mean(x * x, axis=-1, keepdims=True) + 1e-5)
        n = (x * r * gain[...]).astype(BF)
        normed[b] = n
        qkv = dot(n, weights)
        raw[b] = qkv
        q, kv = qkv[:, 0:128], qkv[:, 128:256]
        cos, sin = trig[0, b], trig[1, b]
        qn = q * lax.rsqrt(head_sums(q * q) * (1.0 / 64) + 1e-6) * qk_gain[0:1]
        q_rot = (qn * cos + spin(qn) * sin).astype(BF).astype(F32) * 0.125
        kn = kv * lax.rsqrt(head_sums(kv * kv) * (1.0 / 64) + 1e-6) * qk_gain[1:2]
        k_rot = kn * cos + spin(kn) * sin
        same = jnp.where(segs[b] == docs, 1.0, 0.0)
        doc = dot_tn(same, spot)
        bias = jnp.where((lanes((128, 128)) >= 64) & (lanes((128, 128)) < 72), (doc - 1.0) * NEG, 0.0)
        ones = jnp.where((lanes((128, 128)) >= 72) & (lanes((128, 128)) < 75), 1.0, 0.0)
        kx[b] = jnp.where(low, k_rot, doc + ones).astype(BF)
        one_v = jnp.where((lanes((128, 128)) >= 64) & (lanes((128, 128)) < 67), 1.0, 0.0)
        vx[b] = jnp.where(low, pltpu.roll(kv, 64, 1), one_v).astype(BF)
        q_plain[0, b] = jnp.where(low, q_rot, bias).astype(BF)
        q_plain[1, b] = jnp.where(low, pltpu.roll(q_rot, 64, 1), bias).astype(BF)
        return carry

    lax.fori_loop(0, 8, project, 0)
    k_all = kx[...].reshape(1024, 128)
    v_all = vx[...].reshape(1024, 128)

    def attend(b, carry):
        out = []
        for h in range(2):
            q = q_plain[h, b]
            e = jnp.exp(dot_nt(q, k_all)).astype(BF)
            o = dot(e, v_all)
            total = o[:, 64:65]
            out.append(o / total)
            keep = jnp.where(lanes((128, 128)) >= 72, 0.0, q.astype(F32))
            qx[h, b] = (keep + columns3(-jnp.log(total), 72, (128, 128))).astype(BF)
        both = jnp.where(low, out[0], pltpu.roll(out[1], 64, 1))
        ctx_full[b] = both
        ctx_low[b] = both.astype(BF)
        return carry

    lax.fori_loop(0, 8, attend, 0)


def attend(xs, segs, wps, gain, qk_gain, trig):
    return pl.pallas_call(
        attend_kernel,
        name="attend",
        out_shape=(
            shaped((8, 128, 1024), BF),
            shaped((8, 128, 256), F32),
            shaped((2, 8, 128, 128), BF),
            shaped((8, 128, 128), BF),
            shaped((8, 128, 128), BF),
            shaped((8, 128, 128), F32),
            shaped((8, 128, 128), BF),
        ),
        in_specs=[VM] * 6,
        out_specs=(VM,) * 7,
        scratch_shapes=[pltpu.VMEM((2, 8, 128, 128), BF)],
        compiler_params=local_params(),
    )(xs, segs, wps, gain, qk_gain, trig)


def middle_kernel(ctx, x, wos, gain, middle, ctx_rows, mids, rows, own, ssem, rsem, local):
    p = Place()
    w = Wire(ssem, rsem)
    greet([p.ctx_peer(i) for i in range(1, 8)] + [p.y_up, p.y_dn, p.x_far, p.core])()
    place = pl.ds(pl.multiple_of(p.c * 128, 128), 128)
    keep = pltpu.make_async_copy(ctx.at[p.c], rows.at[:, place], local.at[0])
    keep.start()
    arrivals = []
    for i in range(1, 8):
        to = lax.rem(p.c + i, 8)
        arrivals.append(w.send(ctx.at[to], rows.at[:, place], (to, p.f)))
    keep.wait()
    for copy in arrivals:
        copy.wait_recv()
    for t in range(4):
        cols = slice(256 * t, 256 * t + 256)
        middle[:, cols] = x[:, cols].astype(F32) + dot(rows[...], wos[:, cols])
    m = middle[...]
    r = lax.rsqrt(jnp.mean(m * m, axis=-1, keepdims=True) + 1e-5)
    own[...] = (m * r * gain[...]).astype(BF)
    ctx_rows[...] = rows[...]
    run_all([gather16(w, p, own, mids, 64, local.at[1])])
    w.done()


def middle_gather(ctx, x, wos, gain):
    return pl.pallas_call(
        middle_kernel,
        name="middle_gather",
        out_shape=(
            shaped((128, 1024), F32),
            shaped((128, 1024), BF),
            shaped((16, 128, 1024), BF),
        ),
        in_specs=[ANY, VM, VM, VM],
        out_specs=(VM, VM, ANY),
        scratch_shapes=[
            pltpu.VMEM((128, 1024), BF),
            pltpu.VMEM((128, 1024), BF),
            pltpu.SemaphoreType.DMA((32,)),
            pltpu.SemaphoreType.DMA((32,)),
            pltpu.SemaphoreType.DMA((2,)),
        ],
        compiler_params=remote_params(2),
    )(ctx, x, wos, gain)


LATE_IN = {
    "gs": VM,
    "mids": ANY,
    "cots": ANY,
    "wg": ANY,
    "wu": ANY,
    "wd": ANY,
    "middle": ((128, 1024), F32),
    "x": ((128, 1024), BF),
    "cot": ((128, 1024), BF),
    "wos": ANY,
    "ctx_rows": ((128, 1024), BF),
    "ctx_full": ((8, 128, 128), F32),
    "qx": ((2, 8, 128, 128), BF),
    "kx": ((8, 128, 128), BF),
    "vx": ((8, 128, 128), BF),
    "raw": ((8, 128, 256), F32),
    "normed": ANY,
    "xs": ANY,
    "wps": ((16, 80, 256), BF),
    "trig": ((2, 8, 128, 128), F32),
    "gain_in": VM,
    "gain_mid": VM,
    "qk_gain": VM,
}
LATE_OUT = {
    "output": ((128, 1024), BF, VM),
    "input_grad": ((128, 1024), F32, VM),
    "gu_all": ((2, 8, 128, 1024), BF, ANY),
    "d_all": ((2, 4, 128, 1024), BF, ANY),
    "w_all": ((8, 64, 256), BF, ANY),
    "out_all": ((8, 64, 128), BF, ANY),
    "small_sum": ((24, 128), F32, VM),
}
LATE_SCRATCH = {
    "table": ((32, 128), F32),
    "key": ((32, 128), F32),
    "hot": ((8, 2 * CAP * 2, 256), BF),
    "gate": ((8, 2, 2 * CAP, 128), F32),
    "mid_buf": ((16, 128, 1024), BF),
    "cot_buf": ((16, 128, 1024), BF),
    "wgu": ((2, 8, 128, 1024), BF),
    "wdb": ((8, 128, 1024), BF),
    "xin": ((8, 2, 2 * CAP, 1024), BF),
    "gout": ((8, 2, 2 * CAP, 1024), BF),
    "act": ((16 * CAP, 512), BF),
    "ggu": ((16 * CAP, 1024), BF),
    "dgu": ((2, 8, 128, 1024), BF),
    "ddn": ((2, 4, 128, 1024), BF),
    "ufar": ((2, 2, 128, 1024), BF),
    "unear": ((2, 2, 2, 128, 1024), BF),
    "ulast": ((2, 128, 1024), BF),
    "dx": ((4, 128, 1024), BF),
    "dfar": ((2, 64, 1024), BF),
    "dnear": ((2, 128, 1024), BF),
    "own_d": ((128, 1024), BF),
    "total": ((128, 1024), F32),
    "grad_middle": ((128, 1024), F32),
    "branch": ((128, 1024), BF),
    "back": ((128, 1024), BF),
    "dctx": ((8, 128, 128), BF),
    "gx": ((2, 8, 128, 128), BF),
    "dq": ((2, 1024, 128), F32),
    "dkv": ((8, 128, 128), BF),
    "dqkv": ((8, 128, 256), BF),
    "zfar": ((2, 2, 64, 1024), BF),
    "znear": ((2, 2, 128, 1024), BF),
    "zlast": ((128, 1024), BF),
    "zsend": ((128, 1024), BF),
    "w_own": ((64, 256), BF),
    "out_own": ((8, 64, 128), BF),
    "out_parts": ((7, 64, 128), BF),
    "out_mine": ((64, 128), BF),
    "small": ((24, 128), F32),
    "ctx_small": ((7, 24, 128), F32),
    "mid_small": ((24, 128), F32),
    "fsdp_small": ((16, 24, 128), F32),
}
COPIES = 224
FETCHES = 40


def ring_rows(slot, size):
    return pl.ds(pl.multiple_of(slot * size, size), size)


def late_kernel(*refs):
    names = list(LATE_IN) + list(LATE_OUT) + list(LATE_SCRATCH)
    r = SimpleNamespace(**dict(zip(names, refs)))
    rest = list(refs[len(names) :])
    staged = {n: rest.pop(0) for n, v in LATE_IN.items() if isinstance(v, tuple)}
    red_g, red_o, red_q, red_w = (rest[4 * i : 4 * i + 4] for i in range(4))
    ssem, rsem, lsem = rest[16:]
    p = Place()
    w = Wire(ssem, rsem)
    fetch = Fetch(lsem)
    arrived = greet(
        [p.ctx_peer(i) for i in range(1, 8)] + [p.fsdp_peer(i) for i in range(1, 16)]
    )
    fetch.go("cots", r.cots, r.cot_buf)
    fetch.go("mids", r.mids, r.mid_buf)
    for j in range(2):
        fetch.go("w", r.wg.at[j], r.wgu.at[j, :, :, pl.ds(0, 512)])
        fetch.go("w", r.wu.at[j], r.wgu.at[j, :, :, pl.ds(512, 512)])
    fetch.go("w", r.wd, r.wdb)
    for name, ref in staged.items():
        fetch.go(name, getattr(r, name), ref)
        setattr(r, name, ref)

    for s in range(16):
        r.table[2 * s : 2 * s + 2, :] = r.gs[s, pl.ds(2 * p.f, 2), :]
    named = r.table[...] > 0.0
    row = lax.broadcasted_iota(jnp.int32, (128, 128), 0)
    col = lax.broadcasted_iota(jnp.int32, (128, 128), 1)
    before = jnp.where(row < col, 1.0, 0.0).astype(BF)
    count = dot(jnp.where(named, 1.0, 0.0).astype(BF), before)
    odd = lax.rem(lax.broadcasted_iota(jnp.int32, (32, 128), 0) // 2, 2).astype(F32)
    r.key[...] = jnp.where(named, count + odd * CAP, -1.0)
    slot_id = lax.broadcasted_iota(jnp.int32, (2 * CAP, 256), 0).astype(F32)
    for q in range(8):
        for j in range(2):
            a, b = 4 * q + j, 4 * q + 2 + j
            keys = jnp.concatenate([r.key[a : a + 1, :], r.key[b : b + 1, :]], axis=1)
            vals = jnp.concatenate([r.table[a : a + 1, :], r.table[b : b + 1, :]], axis=1)
            chosen = slot_id == keys
            r.hot[q, 2 * CAP * j : 2 * CAP * (j + 1)] = jnp.where(chosen, 1.0, 0.0).astype(BF)
            weight = jnp.sum(jnp.where(chosen, vals, 0.0), axis=1, keepdims=True)
            r.gate[q, j] = jnp.broadcast_to(weight, (2 * CAP, 128))
    fetch.need("cots")
    for q in range(8):
        rows = dot(r.hot[q], r.cot_buf[2 * q : 2 * q + 2].reshape(256, 1024))
        weight = r.gate[q].reshape(4 * CAP, 128)[:, 0:1]
        r.gout[q] = (weight * rows).astype(BF).reshape(2, 2 * CAP, 1024)
    fetch.need("mids")
    for q in range(8):
        rows = dot(r.hot[q], r.mid_buf[2 * q : 2 * q + 2].reshape(256, 1024))
        r.xin[q] = rows.astype(BF).reshape(2, 2 * CAP, 1024)
    fetch.need("w")

    def expert(j):
        x = r.xin[:, j].reshape(16 * CAP, 1024)
        go = r.gout[:, j].reshape(16 * CAP, 1024)
        w_back = r.wdb[pl.ds(4 * j, 4)].reshape(512, 1024)
        for n in range(2):
            left, right = slice(256 * n, 256 * n + 256), slice(256 * n + 512, 256 * n + 768)
            gp = dot(x, r.wgu[j, :, :, left].reshape(1024, 256))
            up = dot(x, r.wgu[j, :, :, right].reshape(1024, 256))
            ga = dot_nt(go, w_back[left])
            s = 1.0 / (1.0 + jnp.exp(-gp))
            silu = gp * s
            r.act[:, left] = (silu * up).astype(BF)
            r.ggu[:, left] = (ga * up * (s * (1.0 + gp * (1.0 - s)))).astype(BF)
            r.ggu[:, right] = (ga * silu).astype(BF)
        for n in range(4):
            cols = slice(256 * n, 256 * n + 256)
            part = dot_tn(x[:, cols], r.ggu[...]).astype(BF)
            r.dgu[j, 2 * n : 2 * n + 2] = part.reshape(2, 128, 1024)
            r.ddn[j, :, :, cols] = dot_tn(r.act[...], go[:, cols]).astype(BF).reshape(4, 128, 256)
        weight = r.gate[:, j].reshape(16 * CAP, 128)[:, 0:1]
        for n in range(4):
            cols = slice(256 * n, 256 * n + 256)
            part = (weight * dot(r.act[...], w_back[:, cols])).astype(BF)
            r.xin[:, j, :, cols] = part.reshape(8, 2 * CAP, 256)
            part = dot_nt(r.ggu[...], r.wgu[j, 2 * n : 2 * n + 2].reshape(256, 1024))
            r.gout[:, j, :, cols] = part.astype(BF).reshape(8, 2 * CAP, 256)

    theirs, ours = 1 - p.xl, p.xl

    def ring_gu(i, e):
        def mine(d, h):
            return r.dgu.at[e, lax.rem(p.z + d, 4) * 2 + h]

        yield from ring_reduce(
            w,
            p.z_up,
            p.z_dn,
            mine,
            r.ufar.at[i, 0],
            r.ufar.at[i, 1],
            lambda h: r.unear.at[i, 0, h],
            lambda h: r.unear.at[i, 1, h],
        )

    def sum_gu(i, e):
        return (
            r.dgu[e, pl.ds(2 * p.z, 2)].astype(F32)
            + r.unear[i, 0].astype(F32)
            + r.unear[i, 1].astype(F32)
        )

    handed = {}

    def first_gu():
        yield from ring_gu(0, theirs)
        r.unear[0, 0] = sum_gu(0, theirs).astype(BF)
        handed["gu"] = w.send(r.unear.at[0, 0], r.ulast, p.x_near)

    def second_gu():
        yield from ring_gu(1, ours)
        total = sum_gu(1, ours)
        handed["gu"].wait_recv()
        r.ulast[...] = (total + r.ulast[...].astype(F32)).astype(BF)

        def slot(e, dz):
            return r.gu_all.at[e, pl.ds(lax.rem(p.z + dz, 4) * 2, 2)]

        def half(e, dz, h):
            return r.gu_all.at[e, lax.rem(p.z + dz, 4) * 2 + h]

        fetch.go("own_gu", r.ulast, slot(ours, 0))
        rings = [
            (
                w.send(r.ulast, slot(ours, 0), p.z_up),
                w.send(r.ulast, slot(ours, 0), p.z_dn),
                ours,
            )
        ]
        near = w.send(r.ulast, slot(ours, 0), p.x_near)
        yield
        near.wait_recv()
        rings.append(
            (
                w.send(slot(theirs, 0), slot(theirs, 0), p.z_up),
                w.send(slot(theirs, 0), slot(theirs, 0), p.z_dn),
                theirs,
            )
        )
        yield
        halves = []
        for up, down, e in rings:
            up.wait_recv()
            halves.append(w.send(half(e, 3, 0), half(e, 3, 0), p.z_up))
            down.wait_recv()
            halves.append(w.send(half(e, 1, 1), half(e, 1, 1), p.z_dn))
            yield
        for copy in halves:
            copy.wait_recv()
        fetch.need("own_gu")

    def downs():
        copy = w.send(r.ddn.at[theirs], r.dx, p.x_near)
        yield
        copy.wait_recv()
        r.dx[...] = add_low(r.ddn[ours], r.dx[...])
        spans = (pl.ds(0, 64), pl.ds(64, 64))
        ring = ring_reduce(
            w,
            p.z_up,
            p.z_dn,
            lambda d, h: r.dx.at[lax.rem(p.z + d, 4), spans[h]],
            r.dfar.at[0],
            r.dfar.at[1],
            lambda h: r.dnear.at[0, spans[h]],
            lambda h: r.dnear.at[1, spans[h]],
        )
        next(ring)
        yield from ring
        r.own_d[...] = (
            r.dx[p.z].astype(F32) + r.dnear[0].astype(F32) + r.dnear[1].astype(F32)
        ).astype(BF)

        def slot(dz):
            return r.d_all.at[ours, lax.rem(p.z + dz, 4)]

        def half(dz, h):
            return r.d_all.at[ours, lax.rem(p.z + dz, 4), spans[h]]

        fetch.go("own_d", r.own_d, slot(0))
        up = w.send(r.own_d, slot(0), p.z_up)
        down = w.send(r.own_d, slot(0), p.z_dn)
        near = [w.send(r.own_d, slot(0), p.x_near)]
        yield
        up.wait_recv()
        a = w.send(half(3, 0), half(3, 0), p.z_up)
        near.append(w.send(slot(3), slot(3), p.x_near))
        down.wait_recv()
        b = w.send(half(1, 1), half(1, 1), p.z_dn)
        near.append(w.send(slot(1), slot(1), p.x_near))
        yield
        a.wait_recv()
        b.wait_recv()
        near.append(w.send(slot(2), slot(2), p.x_near))
        yield
        for copy in near:
            copy.wait_recv()
        fetch.need("own_d")

    def combine(rows, out):
        def produce(slot):
            q = slot // 2
            both = dot_tn(r.hot[q], rows[q].reshape(4 * CAP, 1024))
            out[pl.ds(2 * q, 2)] = both.astype(BF).reshape(2, 128, 1024)

        return produce

    def keep_total(v):
        r.total[...] = v

    def write_output(v):
        r.output[...] = (r.middle[...] + v).astype(BF)

    gm = reduce16(w, p, lambda slot: r.cot_buf.at[slot], *red_g, keep_total, combine(r.gout, r.cot_buf))
    outs = reduce16(w, p, lambda slot: r.mid_buf.at[slot], *red_o, write_output, combine(r.xin, r.mid_buf))
    a, b, d = first_gu(), second_gu(), downs()

    arrived()
    expert(theirs)
    next(d)
    next(a)
    next(a)
    expert(ours)
    fetch.go("wos", r.wos, r.wgu.at[0])
    fetch.go("normed", r.normed, r.wgu.at[1])
    next(a)
    next(b)
    next(b)
    next(gm)
    next(d)
    fetch.need("middle")
    next(outs)
    next(gm)
    for _ in a:
        pass
    next(gm)
    next(outs)
    next(b)
    next(gm)
    next(d)
    for _ in gm:
        pass

    fetch.need("cot", "wos", "ctx_rows")
    m = r.middle[...]
    gy = r.total[...] * r.gain_mid[...]
    rm = lax.rsqrt(jnp.mean(m * m, axis=-1, keepdims=True) + 1e-5)
    inner = jnp.mean(gy * m, axis=-1, keepdims=True)
    gmid = r.cot[...].astype(F32) + rm * gy - m * (rm * rm * rm * inner)
    r.grad_middle[...] = gmid
    gain_sum = jnp.sum(r.total[...] * (m * rm), axis=0, keepdims=True)
    for i in range(8):
        r.small[8 + i : 9 + i, :] = gain_sum[:, 128 * i : 128 * i + 128]
    r.branch[...] = gmid.astype(BF)
    r.back[...] = dot_nt(r.branch[...], r.wgu[0].reshape(1024, 1024)).astype(BF)
    fetch.go("xs", r.xs, r.wgu.at[0])
    place = ring_rows(p.c, 128)
    fetch.go("dctx", r.back.at[:, place], r.dctx.at[p.c])
    arrivals = []
    for i in range(1, 8):
        to = lax.rem(p.c + i, 8)
        arrivals.append(w.send(r.back.at[:, ring_rows(to, 128)], r.dctx.at[p.c], (to, p.f)))
    next(outs)
    for n in range(4):
        part = dot_tn(r.ctx_rows[:, 256 * n : 256 * n + 256], r.branch[...]).astype(BF)
        r.xin[2 * n : 2 * n + 2, :, 0:64, :] = part.reshape(2, 2, 64, 1024)

    def grad_out(slot):
        return r.xin.at[slot // 2, lax.rem(slot, 2), pl.ds(0, 64)]

    def grad_w(slot):
        return r.gout.at[slot // 2, lax.rem(slot, 2), pl.ds(0, 64), pl.ds(0, 256)]


    def out_weight():
        def finish(v):
            for i in range(8):
                r.out_own[i] = v[:, 128 * i : 128 * i + 128].astype(BF)

        yield from reduce16(w, p, grad_out, *red_q, finish)
        arrivals = []
        for i in range(1, 8):
            to = lax.rem(p.c + i, 8)
            arrivals.append(w.send(r.out_own.at[to], r.out_parts.at[i - 1], (to, p.f)))
        yield
        sums = r.out_own[p.c].astype(F32)
        for i, copy in enumerate(arrivals):
            copy.wait_recv()
            sums = sums + r.out_parts[i].astype(F32)
        r.out_mine[...] = sums.astype(BF)
        yield
        yield from spread(r.out_mine, r.out_all, "out_mine")

    def spread(own, out, name):
        fetch.go(name, own, out.at[p.c])
        copies = [w.send(own, out.at[p.c], p.ctx_peer(i)) for i in range(1, 8)]
        yield
        for copy in copies:
            copy.wait_recv()
        fetch.need(name)

    ow = out_weight()
    next(ow)
    for copy in arrivals:
        copy.wait_recv()
    fetch.need("dctx", "ctx_full", "qx", "kx", "vx")

    low = lanes((128, 128)) < 64

    def prepare(b, carry):
        d = r.dctx[b].astype(F32)
        prod = d * r.ctx_full[b]
        left = jnp.sum(jnp.where(low, prod, 0.0), axis=-1, keepdims=True)
        right = jnp.sum(jnp.where(low, 0.0, prod), axis=-1, keepdims=True)
        r.gx[0, b] = jnp.where(low, d, columns3(-left, 64, (128, 128))).astype(BF)
        r.gx[1, b] = jnp.where(
            low, pltpu.roll(d, 64, 1), columns3(-right, 64, (128, 128))
        ).astype(BF)
        return carry

    lax.fori_loop(0, 8, prepare, 0)

    def block(i):
        at = slice(2 * i, 2 * i + 2)
        k = r.kx[at].reshape(256, 128)
        v = r.vx[at].reshape(256, 128)
        grad_k = jnp.zeros((256, 128), F32)
        grad_v = jnp.zeros((256, 128), F32)
        for h in range(2):
            q_all = r.qx[h].reshape(1024, 128)
            g_all = r.gx[h].reshape(1024, 128)
            pt = jnp.exp(dot_nt(k, q_all))
            dst = (pt * dot_nt(v, g_all)).astype(BF)
            grad_v = grad_v + dot(pt.astype(BF), g_all)
            grad_k = grad_k + dot(dst, q_all)
            part = dot_tn(dst, k)
            r.dq[h] = part if i == 0 else r.dq[h] + part
        both = jnp.where(lanes((256, 128)) < 64, grad_k, pltpu.roll(grad_v, 64, 1))
        r.dkv[at] = both.astype(BF).reshape(2, 128, 128)

    block(0)
    next(b)
    next(outs)
    block(1)
    next(ow)
    for _ in outs:
        pass
    block(2)
    next(d)
    next(ow)
    block(3)
    next(b)
    next(ow)
    fetch.need("raw", "wps", "trig", "xs", "normed", "x")

    weights = r.wps[:, 0:64, :].reshape(1024, 256)
    sums = [jnp.zeros((1, 1024), F32), jnp.zeros((1, 128), F32), jnp.zeros((1, 128), F32)]

    def finish(b):
        rows = ring_rows(b, 128)
        cos, sin = r.trig[0, b], r.trig[1, b]
        gq = jnp.where(low, r.dq[0, rows, :], pltpu.roll(r.dq[1, rows, :], 64, 1)) * 0.125
        gq = gq.astype(BF).astype(F32)
        gkv = r.dkv[b].astype(F32)
        gq = gq * cos - spin(gq) * sin
        gkv_rot = gkv * cos - spin(gkv) * sin
        q, kv = r.raw[b, :, 0:128], r.raw[b, :, 128:256]
        rq = lax.rsqrt(head_sums(q * q) * (1.0 / 64) + 1e-6)
        rk = lax.rsqrt(head_sums(kv * kv) * (1.0 / 64) + 1e-6)
        sums[1] = sums[1] + jnp.sum(gq * q * rq, axis=0, keepdims=True)
        sums[2] = sums[2] + jnp.sum(gkv_rot * kv * rk, axis=0, keepdims=True)
        gq = gq * r.qk_gain[0:1]
        gk = gkv_rot * r.qk_gain[1:2]
        gq = rq * gq - q * (rq * rq * rq) * (head_sums(gq * q) * (1.0 / 64))
        gk = rk * gk - kv * (rk * rk * rk) * (head_sums(gk * kv) * (1.0 / 64))
        gkv = jnp.where(low, gk, gkv)
        r.dqkv[b, :, 0:128] = gq.astype(BF)
        r.dqkv[b, :, 128:256] = gkv.astype(BF)
        gn = dot_nt(r.dqkv[b], weights)
        partial[b] = gn.astype(BF)
        x = r.wgu[0, b].astype(F32)
        rx = lax.rsqrt(jnp.mean(x * x, axis=-1, keepdims=True) + 1e-5)
        sums[0] = sums[0] + jnp.sum(gn * (x * rx), axis=0, keepdims=True)

    partial = r.wdb
    halves = (pl.ds(0, 64), pl.ds(64, 64))
    ring = ring_reduce(
        w,
        p.z_up,
        p.z_dn,
        lambda d, h: partial.at[pl.ds(lax.rem(p.z + d, 4) * 2, 2), halves[h]],
        r.zfar.at[0],
        r.zfar.at[1],
        lambda h: r.znear.at[0, :, halves[h]],
        lambda h: r.znear.at[1, :, halves[h]],
    )
    for dz in (2, 1, 3, 0):
        for e in (0, 1):
            finish(lax.rem(p.z + dz, 4) * 2 + e)
        if dz == 2:
            next(ring)
        if dz == 3:
            next(ring)

    def tokens():
        yield from ring

        def summed(e):
            return (
                partial[2 * p.z + e].astype(F32)
                + r.znear[0, e].astype(F32)
                + r.znear[1, e].astype(F32)
            )

        r.zsend[...] = summed(theirs).astype(BF)
        copy = w.send(r.zsend, r.zlast, p.x_near)
        yield
        total = summed(ours)
        copy.wait_recv()
        gy = (total + r.zlast[...].astype(F32)) * r.gain_in[...]
        v = r.x[...].astype(F32)
        rx = lax.rsqrt(jnp.mean(v * v, axis=-1, keepdims=True) + 1e-5)
        inner = jnp.mean(gy * v, axis=-1, keepdims=True)
        r.input_grad[...] = r.grad_middle[...] + rx * gy - v * (rx * rx * rx * inner)

    def projections():
        def keep(v):
            r.w_own[...] = v.astype(BF)

        yield from reduce16(w, p, grad_w, *red_w, keep)
        yield from spread(r.w_own, r.w_all, "w_own")

    def vectors():
        first = [w.send(r.small, r.ctx_small.at[i - 1], p.ctx_peer(i)) for i in range(1, 8)]
        yield
        total = r.small[...]
        for i, copy in enumerate(first):
            copy.wait_recv()
            total = total + r.ctx_small[i]
        r.mid_small[...] = total
        r.fsdp_small[p.f] = total
        second = [
            w.send(r.mid_small, r.fsdp_small.at[p.f], p.fsdp_peer(i)) for i in range(1, 16)
        ]
        yield
        for copy in second:
            copy.wait_recv()
        total = r.fsdp_small[0]
        for i in range(1, 16):
            total = total + r.fsdp_small[i]
        r.small_sum[...] = total

    norm_sum, q_sum, k_sum = sums
    for i in range(8):
        r.small[i : i + 1, :] = norm_sum[:, 128 * i : 128 * i + 128]
    q_sum = q_sum + pltpu.roll(q_sum, 64, 1)
    k_sum = jnp.where(lanes((1, 128)) < 64, q_sum, pltpu.roll(k_sum, 64, 1))
    r.small[16:24, :] = jnp.broadcast_to(k_sum, (8, 128))
    vec = vectors()
    next(vec)
    part = dot_tn(r.wgu[1].reshape(1024, 1024), r.dqkv[...].reshape(1024, 256))
    r.gout[:, :, 0:64, 0:256] = part.astype(BF).reshape(8, 2, 64, 256)
    pw = projections()
    next(pw)
    run_all([tokens(), pw, vec, ow, b, d])
    w.done()


def late(**given):
    staged = [v for v in LATE_IN.values() if isinstance(v, tuple)]
    in_specs = [ANY if isinstance(v, tuple) else v for v in LATE_IN.values()]
    return pl.pallas_call(
        late_kernel,
        name="late",
        out_shape=tuple(shaped(v[0], v[1]) for v in LATE_OUT.values()),
        in_specs=in_specs,
        out_specs=tuple(v[2] for v in LATE_OUT.values()),
        scratch_shapes=[pltpu.VMEM(*v) for v in LATE_SCRATCH.values()]
        + [pltpu.VMEM(*v) for v in staged]
        + reduce16_scratch(128, 1024)
        + reduce16_scratch(128, 1024)
        + reduce16_scratch(64, 1024)
        + reduce16_scratch(64, 256)
        + [
            pltpu.SemaphoreType.DMA((COPIES,)),
            pltpu.SemaphoreType.DMA((COPIES,)),
            pltpu.SemaphoreType.DMA((FETCHES,)),
        ],
        compiler_params=remote_params(3),
    )(*[given[n] for n in LATE_IN])


def trig_tables():
    index = np.arange(1024)
    stored = index // 64
    natural = np.where(stored % 2 == 0, stored // 2, 15 - stored // 2)
    pos = (natural * 64 + index % 64).astype(np.float32)
    freq = (10000.0 ** (-np.arange(32) * 2.0 / 64)).astype(np.float32)
    angle = (pos[:, None] * freq[None, :]).astype(np.float64)
    cos, sin = np.cos(angle), np.sin(angle)
    cos = np.concatenate([cos] * 4, axis=1)
    sin = np.concatenate([-sin, sin, -sin, sin], axis=1)
    return np.stack([cos, sin]).astype(np.float32).reshape(2, 8, 128, 128)


def on_device(
    inputs, segments, routes, gate_weights, cotangent, norm_in, norm_mid, q_gain, k_gain,
    w_query, w_key, w_value, w_out, w_gate, w_up, w_down,
):
    c = lax.axis_index("ctx")
    f = lax.axis_index("fsdp")
    x, cot = inputs[0], cotangent[0]
    trig = jnp.asarray(trig_tables())
    wp = jnp.concatenate(
        [
            lax.dynamic_slice(w_query, (0, 128 * c), (64, 128)),
            lax.dynamic_slice(w_key, (0, 64 * c), (64, 64)),
            lax.dynamic_slice(w_value, (0, 64 * c), (64, 64)),
        ],
        axis=1,
    )
    gains = jnp.pad(jnp.concatenate([norm_in, norm_mid])[None], ((0, 15), (0, 128)))
    wp = jnp.concatenate([wp, gains], axis=0)
    seg = jnp.broadcast_to(segments, (8, 128))
    expert_ids = jnp.arange(EXPERTS, dtype=jnp.int32)
    g = jnp.sum(
        jnp.where(
            routes[0].T[None, :, :] == expert_ids[:, None, None], gate_weights[0].T[None], 0.0
        ),
        axis=1,
    )
    ones = jnp.ones((64,), F32)
    qk_gain = jnp.stack(
        [
            jnp.concatenate([q_gain, q_gain]).astype(F32),
            jnp.concatenate([k_gain.astype(F32), ones]),
        ]
    )
    xs, segs, wps, wos, gs, cots = first_gather(x, seg, wp, w_out, g, cot)
    gain_in = wps[:, 64, 0:64].reshape(1, 1024).astype(F32)
    gain_mid = wps[:, 64, 64:128].reshape(1, 1024).astype(F32)
    wo_full = wos.reshape(1024, 1024)
    normed, raw, qx, kx, vx, ctx_full, ctx_low = attend(xs, segs, wps, gain_in, qk_gain, trig)
    middle, ctx_rows, mids = middle_gather(ctx_low, x, wo_full, gain_mid)
    output, input_grad, gu_all, d_all, w_all, out_all, small_sum = late(
        gs=gs,
        mids=mids,
        cots=cots,
        wg=w_gate.reshape(2, 8, 128, 512),
        wu=w_up.reshape(2, 8, 128, 512),
        wd=w_down.reshape(8, 128, 1024),
        middle=middle,
        x=x,
        cot=cot,
        wos=wos.reshape(8, 128, 1024),
        ctx_rows=ctx_rows,
        ctx_full=ctx_full,
        qx=qx,
        kx=kx,
        vx=vx,
        raw=raw,
        normed=normed,
        xs=xs,
        wps=wps,
        trig=trig,
        gain_in=gain_in,
        gain_mid=gain_mid,
        qk_gain=qk_gain,
    )
    gu = gu_all.reshape(2, 1024, 1024)
    grad_wq = w_all[:, :, 0:128].transpose(1, 0, 2).reshape(64, 1024).astype(F32)
    grad_wk = w_all[:, :, 128:192].transpose(1, 0, 2).reshape(64, 512).astype(F32)
    grad_wv = w_all[:, :, 192:256].transpose(1, 0, 2).reshape(64, 512).astype(F32)
    grad_wo = out_all.transpose(1, 0, 2).reshape(64, 1024).astype(F32)
    grad_norm_in = lax.dynamic_slice(small_sum[0:8].reshape(1024), (64 * f,), (64,))
    grad_norm_mid = lax.dynamic_slice(small_sum[8:16].reshape(1024), (64 * f,), (64,))
    return (
        output[None],
        input_grad[None],
        grad_norm_in,
        grad_norm_mid,
        small_sum[16, 0:64],
        small_sum[16, 64:128],
        grad_wq,
        grad_wk,
        grad_wv,
        grad_wo,
        gu[:, :, :512].astype(F32),
        gu[:, :, 512:].astype(F32),
        d_all.reshape(2, 512, 1024).astype(F32),
    )


def solution(mesh):
    rows = P("fsdp", "ctx", None)
    in_specs = (
        rows,
        P("fsdp", "ctx"),
        rows,
        rows,
        rows,
        P("fsdp"),
        P("fsdp"),
        P(),
        P(),
        P("fsdp", None),
        P("fsdp", None),
        P("fsdp", None),
        P("fsdp", None),
        P("fsdp", None, None),
        P("fsdp", None, None),
        P("fsdp", None, None),
    )
    out_specs = (
        rows,
        rows,
        P("fsdp"),
        P("fsdp"),
        P(),
        P(),
        P("fsdp", None),
        P("fsdp", None),
        P("fsdp", None),
        P("fsdp", None),
        P("fsdp", None, None),
        P("fsdp", None, None),
        P("fsdp", None, None),
    )
    return jax.shard_map(
        on_device, mesh=mesh, in_specs=in_specs, out_specs=out_specs, check_vma=False
    )
```

time: 351 us -> 290 us (0.83)
  Pallas kernels: 319 us -> 257 us
    pallas_call x4 -> x1, Pallas kernels: 225 us -> 163 us  [late(): pl.pallas_call(late_kernel, name='late', out_shape=tuple((shaped(v[0], v[...]
    convert_element_type x3 -> x2, other arithmetic: 7.7 us -> 7.4 us  [the longest x1 4.66 us: on_device(): gu[:, :, 512:].astype(F32)]
where the time goes in v2:
time: 290 us; the launch traced here: 286 us
  Pallas kernels  257 us (89%)
  other arithmetic  16.9 us (6%)
  local copies, waits for them, and re-layouts  11.7 us (4%)
    pallas_call x1, Pallas kernels, late(): pl.pallas_call(late_kernel, name='late', out_shape=tuple((shaped(v[0], v[...  163 us
    pallas_call x1, Pallas kernels, first_gather(): pl.pallas_call(first_kernel, name='first_gather', out_shape=(shaped((8,)...  45.1 us
    pallas_call x1, Pallas kernels, middle_gather(): pl.pallas_call(middle_kernel, name='middle_gather', out_shape=(shaped((12...  34.1 us
    pallas_call x1, Pallas kernels, attend(): pl.pallas_call(attend_kernel, name='attend', out_shape=(shaped((8, 128, 1...  14.8 us

profile of v2, /device:TPU:0, one launch (start us, length us, event | category | flops | bytes accessed | tf_op | source)
XLA Modules:
  0.0 286.4 jit_solution(16633195135647602171)
XLA Ops:
  0.6 0.0 copy-start
  0.7 0.8 maximum_bitcast_fusion
  1.4 0.7 pad_bitcast_fusion
  2.1 1.4 maximum_convert_fusion.qk_gain.refs_22_
  3.5 1.2 broadcast_in_dim.33.seg
  4.7 0.0 copy-done
  4.8 1.4 select_reduce_fusion.g
  6.1 0.8 constant_dynamic-slice_fusion
  6.9 0.7 fusion.1.wp
  7.6 45.1 %first_gather.1 = (bf16[8,128,1024]{2,1,0:T(8,128)(2,1)}, s32[8,8,128]{2,1,0:T(8,128)}, bf16[16,80,256]{2,1,0:T(8,128)(2,1)}, bf16[16,64,1024]{2,1,0:T(8,128)(2,...) custom-call(bf16[128,1024]{1,0:T(8,128)(2,1)} %bitcast.52, s32[8,128]{1,0:T(8,128)} %broadcast_in_dim.33.seg, ...), custom_call_target="tpu_custom_call" | custom-call | tf_op jit(solution)/shard_map/first_gather/pallas_call | solution.py:291
  52.7 0.9 convert_reduce_fusion
  53.7 0.7 reshape.133.gain.refs_21_
  54.3 0.7 reshape.132.gain.refs_20_
  55.0 14.8 %attend.1 = (bf16[8,128,1024]{2,1,0:T(8,128)(2,1)}, f32[8,128,256]{2,1,0:T(8,128)}, bf16[2,8,128,128]{3,2,1,0:T(8,128)(2,1)}, bf16[8,128,128]{2,1,0:T(8,128)(2,1...) custom-call(bf16[8,128,1024]{2,1,0:T(8,128)(2,1)} %get-tuple-element.37.xs.refs_17_, ...), custom_call_target="tpu_custom_call" | custom-call | tf_op jit(solution)/shard_map/attend/pallas_call | solution.py:400
  69.8 34.1 %middle_gather.1 = (f32[128,1024]{1,0:T(8,128)}, bf16[128,1024]{1,0:T(8,128)(2,1)}, bf16[16,128,1024]{2,1,0:T(8,128)(2,1)}) custom-call(bf16[8,128,128]{2,1,0:T(8,128)(2,1)} %get-tuple-element.40.ctx, bf16[128,1024]{1,0:T(8,128)(2,1)} %bitcast.53, bf16[1024,1024]{1,0:T(8,128)(2,1)} %bitcast.49, f32[1,1024]{1,0:T(1,128)} %reshape.133.gain.refs_21_), custom_call_target="tpu_custom_call" | custom-call | tf_op jit(solution)/shard_map/middle_gather/pallas_call | solution.py:445
  104.0 162.9 %late.1 = (bf16[128,1024]{1,0:T(8,128)(2,1)}, f32[128,1024]{1,0:T(8,128)}, bf16[2,8,128,1024]{3,2,1,0:T(8,128)(2,1)}, bf16[2,4,128,1024]{3,2,1,0:T(8,128)(2,1)},...) custom-call(f32[16,32,128]{2,1,0:T(8,128)} %get-tuple-element.36.refs_0_, ...), custom_call_target="tpu_custom_call" | custom-call | tf_op jit(solution)/shard_map/late/pallas_call | solution.py:1025
  266.9 0.0 copy-start.2
  266.9 1.4 slice_bitcast_fusion.2
  268.3 0.7 slice_bitcast_fusion
  269.0 0.6 dynamic_slice.19
  269.6 0.6 dynamic_slice.18
  270.2 1.6 copy_bitcast_fusion
  271.8 1.6 copy_bitcast_fusion.1
  273.4 1.1 convert_bitcast_fusion.1
  274.5 0.2 copy.36
  274.7 0.8 reshape.136
  275.4 0.2 copy.35
  275.6 0.8 reshape.135
  276.4 0.0 copy-done.2
  276.4 0.0 copy-start.1
  276.4 2.7 bitcast_convert_fusion
  279.1 1.0 copy-done.1
  280.1 0.0 copy-start.4
  280.1 0.0 copy-start.3
  280.1 4.7 %slice_convert_fusion = (f32[2,1024,512]{2,1,0:T(8,128)}, f32[2,1024,512]{2,1,0:T(8,128)}) fusion(bf16[2,1024,1024]{2,1,0:T(8,128)(2,1)S(1)} %bitcast.51), kind=kLoop, calls=%fused_computation | loop fusion | flops 2097152 | bytes 12582912 | tf_op jit(solution)/shard_map/convert_element_type | solution.py:1142
  284.7 0.0 copy-done.4
  284.7 0.7 copy.44
  285.5 0.0 copy-done.3
  285.5 0.8 copy.45
  (1 shorter events, 0.0 us)
Async XLA Ops:
  0.6 4.1 %copy-start = (bf16[64,1024]{1,0:T(8,128)(2,1)S(1)}, bf16[64,1024]{1,0:T(8,128)(2,1)}, u32[]{:S(2)}) copy-start(bf16[64,1024]{1,0:T(8,128)(2,1)} %param.26) | copy-start | bytes 393220
  266.9 9.5 %copy-start.2 = (bf16[2,4,128,1024]{3,2,1,0:T(8,128)(2,1)S(1)}, bf16[2,4,128,1024]{3,2,1,0:T(8,128)(2,1)}, u32[]{:S(2)}) copy-start(bf16[2,4,128,1024]{3,2,1,0:T(8,128)(2,1)} %get-tuple-element.58) | copy-start | bytes 6291460
  276.4 3.7 %copy-start.1 = (bf16[2,8,128,1024]{3,2,1,0:T(8,128)(2,1)S(1)}, bf16[2,8,128,1024]{3,2,1,0:T(8,128)(2,1)}, u32[]{:S(2)}) copy-start(bf16[2,8,128,1024]{3,2,1,0:T(8,128)(2,1)} %get-tuple-element.57) | copy-start | bytes 12582916
  280.1 4.7 %copy-start.4 = (bf16[128,1024]{1,0:T(8,128)(2,1)S(1)}, bf16[128,1024]{1,0:T(8,128)(2,1)}, u32[]{:S(2)}) copy-start(bf16[128,1024]{1,0:T(8,128)(2,1)} %get-tuple-element.52) | copy-start | bytes 786436
  280.1 5.4 %copy-start.3 = (f32[128,1024]{1,0:T(8,128)S(1)}, f32[128,1024]{1,0:T(8,128)}, u32[]{:S(2)}) copy-start(f32[128,1024]{1,0:T(8,128)} %get-tuple-element.53) | copy-start | bytes 1572868
